TPU v7x, 32 devices: a whole 2x2x4 slice. The times are simulated.
32 devices in a mesh: row: 8 (over y, x, core), col: 4 (over z).
Axes of the slice: x: 2, y: 2, z: 4, core: 2. Of those that a mesh axis runs over, the one named last changes fastest.
Arguments:
- hidden: bfloat16 [3072, 5120], P('row', 'col'), may hold values from -6 to 6
- modulation: float32 [2, 5120], replicated, may hold values from -3 to 3
- w_query: bfloat16 [5120, 5120], P('row', 'col'), may hold values from -2 to 2
- w_key: bfloat16 [5120, 5120], P('row', 'col'), may hold values from -2 to 2
- w_value: bfloat16 [5120, 5120], P('row', 'col'), may hold values from -0.078125 to 0.078125
- q_gain: float32 [5120], P('col'), may hold values from 0.4 to 4.3
- k_gain: float32 [5120], P('col'), may hold values from 0.4 to 4.3
- positions: int32 [3, 3072], P(None, 'row'), may hold values from 0 to 63
- segment_ids: int32 [3072], replicated, may hold values from 0 to 11, never falling along the last dimension, each value on 1 to 1536 neighbouring positions
- page_table: int32 [24], replicated, may hold values from 0 to 23, each once
Outputs:
- attended: bfloat16 [3072, 5120], P('row', 'col')
- page_store: bfloat16 [2, 24, 128, 5120], P(None, 'row', None, 'col')
Inputs may be any that keep to these rules, and one draw needn't show every extreme that they name: `segment_ids`: segment numbers never fall along the tokens; each segment holds at most 1536 tokens, and one holds exactly 1536. `page_table`: every slot is named by exactly one block.
All inputs are finite; a program needn't handle non-finite values.
Results may differ from a plain program's by a relative error of at most 0.015.
Values may be sent and summed in bfloat16 or wider, within the bound.
No kernel may reach another device: no remote copies, remote signals or barrier semaphores. Data moves between devices by JAX's collectives and lax.ppermute only.
A program may use at most 128 MiB of HBM per device.

v0:
```python
import functools
import jax
import jax.numpy as jnp
from jax import lax
from jax.experimental import pallas as pl
from jax.experimental.pallas import tpu as pltpu
from jax.sharding import PartitionSpec as P

HEAD_DIM = 128
PAGE = 128
KEY_TILE = 512
VMEM = 60 * 1024 * 1024
LOG2E = 1.4426950408889634

epsilon = 1e-06


def rotary_lanes(positions, head_dim):
    pair_count = head_dim // 2
    frame_pairs = pair_count - 2 * (pair_count // 3)
    side_pairs = pair_count // 3
    column = jnp.arange(head_dim) // 2
    frame_rate = 10000.0 ** (-column.astype(jnp.float32) / frame_pairs)
    height_rate = 10000.0 ** (-(column - frame_pairs).astype(jnp.float32) / side_pairs)
    width_rate = 10000.0 ** (-(column - frame_pairs - side_pairs).astype(jnp.float32) / side_pairs)
    coords = positions.astype(jnp.float32)
    angles = jnp.where(
        column < frame_pairs,
        coords[0][:, None] * frame_rate,
        jnp.where(
            column < frame_pairs + side_pairs,
            coords[1][:, None] * height_rate,
            coords[2][:, None] * width_rate,
        ),
    )
    sine = jnp.sin(angles)
    even = (jnp.arange(head_dim) % 2 == 0)[None, :]
    return jnp.cos(angles), jnp.where(even, -sine, 0.0), jnp.where(even, 0.0, sine)


def modulate(activations, modulation):
    average = jnp.mean(activations, axis=1, keepdims=True)
    centred = activations - average
    variance = jnp.mean(centred * centred, axis=1, keepdims=True)
    normed = centred * lax.rsqrt(variance + epsilon)
    return (normed * (1.0 + modulation[1]) + modulation[0]).astype(jnp.bfloat16)


def cut_kernel(half_ref, *refs):
    weights, outs, sems = refs[:3], refs[3:6], refs[6]
    cols = outs[0].shape[2]
    half = half_ref[0]
    copies = []
    for number, weight in enumerate(weights):
        send, at = (1, number) if number < 2 else (2, 0)
        for which, target in ((half, outs[0].at[number]), (1 - half, outs[send].at[at])):
            span = pl.ds(pl.multiple_of(which * cols, cols), cols)
            copies.append(
                pltpu.make_async_copy(
                    weight.at[:, span], target, sems.at[number, len(copies) % 2]
                )
            )
            copies[-1].start()
    for copy in copies:
        copy.wait()


def cut(weights, half):
    rows, width = weights[0].shape
    cols = width // 2
    whole = pl.BlockSpec(memory_space=pltpu.VMEM)
    return pl.pallas_call(
        cut_kernel,
        in_specs=[pl.BlockSpec(memory_space=pltpu.SMEM)] + [pl.BlockSpec(memory_space=pl.ANY)] * 3,
        out_specs=[whole] * 3,
        out_shape=[jax.ShapeDtypeStruct((size, rows, cols), jnp.bfloat16) for size in (3, 2, 1)],
        scratch_shapes=[pltpu.SemaphoreType.DMA((3, 2))],
        compiler_params=pltpu.CompilerParams(vmem_limit_bytes=VMEM),
        cost_estimate=pl.CostEstimate(
            flops=0, bytes_accessed=12 * rows * width, transcendentals=0
        ),
        name="cut",
    )(half.reshape(1), *weights)


def turned(values, gain, tables, at):
    dim = tables[0].shape[1]
    cols = slice(at * dim, (at + 1) * dim)
    own, upper, lower = tables
    part = values[:, cols] * gain[:, cols]
    return part * own + pltpu.roll(part, dim - 1, 1) * upper + pltpu.roll(part, 1, 1) * lower


def project_kernel(
    parts, blocks, spots, first, final, in_count, place_ref, stats_ref, modulation_ref, *refs
):
    shard_count = sum(len(part[1]) for part in parts)
    out_count = len(refs) - 6 - in_count
    shards, rest = refs[:shard_count], refs[shard_count:]
    total, raws, weights, ready, raw_sems, weight_sems = rest[-6:]
    outs, sources = rest[-6 - out_count : -6], rest[: -6 - out_count]
    if final:
        sources, (gain_ref, own_ref, upper_ref, lower_ref) = sources[:-4], sources[-4:]
    if not first:
        sources, partial_ref = sources[:-1], sources[-1]
    me, rank = place_ref[0], place_ref[1]
    feats, cols = weights.shape[2:]
    rows = raws.shape[1]
    per_rank = shards[0].shape[-1] // feats
    copies = {}
    for slot, block in enumerate(blocks):
        owner = me ^ block
        span = pl.ds(pl.multiple_of((owner % per_rank) * feats, feats), feats)
        holder = owner // per_rank
        mine, begin, at = [], 0, 0
        for number, (length, places, by_rank) in enumerate(parts):
            held = shards[at : at + len(places)]
            at += len(places)
            target = raws.at[slot, pl.ds(begin, length), :]
            begin += length
            sem = raw_sems.at[slot, number]
            if by_rank:
                copy = pltpu.make_async_copy(
                    held[0].at[holder, pl.ds(places[0], length), span], target, sem
                )
                copy.start()
            else:
                for step, (ref, skip) in enumerate(zip(held, places)):
                    source = ref.at[pl.ds(skip, length), span]

                    @pl.when((holder ^ rank) == step)
                    def _(source=source, target=target, sem=sem):
                        pltpu.make_async_copy(source, target, sem).start()

                copy = pltpu.make_async_copy(source, target, sem)
            mine.append(copy)
        matrices = [
            pltpu.make_async_copy(
                sources[source].at[place], weights.at[slot, number], weight_sems.at[slot, number]
            )
            for number, (source, place) in enumerate(spots[block])
        ]
        for copy in matrices:
            copy.start()
        copies[slot] = (mine, matrices)

    def column(at):
        return jnp.transpose(jnp.broadcast_to(stats_ref[at : at + 1, :], (128, rows)))

    mean, scale = column(0), column(1)

    def prepare(first_slot):
        for slot in (first_slot, first_slot + 1):
            for copy in copies[slot][0]:
                copy.wait()
            span = pl.ds(pl.multiple_of((me ^ blocks[slot]) * feats, feats), feats)
            shift = modulation_ref[0:1, span]
            gain = 1.0 + modulation_ref[1:2, span]
            left = (slot - first_slot) * feats
            for start in range(0, feats, 128):
                lanes = slice(start, start + 128)
                part = raws[slot, :, lanes].astype(jnp.float32)
                part = (part - mean) * scale * gain[:, lanes] + shift[:, lanes]
                ready[first_slot // 2 % 2, :, left + start : left + start + 128] = part.astype(
                    jnp.bfloat16
                )

    prepare(0)
    for slot in range(0, len(blocks), 2):
        for copy in copies[slot][1] + copies[slot + 1][1]:
            copy.wait()
        if slot + 2 < len(blocks):
            prepare(slot + 2)
        right = jnp.concatenate(
            [
                jnp.concatenate([weights[slot, m], weights[slot + 1, m]], axis=0)
                for m in range(3)
            ],
            axis=1,
        )
        part = jnp.dot(ready[slot // 2 % 2], right, preferred_element_type=jnp.float32)
        if slot:
            part = part + total[...]
        elif not first:
            part = part + partial_ref[...]
        if slot + 2 < len(blocks):
            total[...] = part
    if not final:
        outs[0][...] = part
        return
    query_ref, squares_ref = outs[:2]
    key_ref, value_ref = outs[2:] if len(outs) == 4 else (outs[2], outs[2])
    key, value, query = [part[:, m * cols : (m + 1) * cols] for m in range(3)]
    query_ref[...] = query
    value_ref[value_ref.shape[0] - 1] = value.astype(jnp.bfloat16)
    tables = (own_ref[...], upper_ref[...], lower_ref[...])
    for head in range(cols // HEAD_DIM):
        lanes = slice(head * HEAD_DIM, (head + 1) * HEAD_DIM)
        key_ref[0, :, lanes] = turned(key, gain_ref, tables, head).astype(jnp.bfloat16)
    for kind, raw in enumerate((key, query)):
        summed = jnp.sum(raw * raw, axis=1, keepdims=True)
        summed = jnp.transpose(jnp.broadcast_to(summed, (rows, 128)))
        squares_ref[kind : kind + 1, :] = summed[:1]


def project(
    place, stats, modulation, parts, blocks, shards, spots, sources, partial, finish, joint=True
):
    rows = sum(part[0] for part in parts)
    _, feats, cols = sources[0].shape
    count = len(blocks)
    anywhere = pl.BlockSpec(memory_space=pl.ANY)
    whole = pl.BlockSpec(memory_space=pltpu.VMEM)
    out_shape = [jax.ShapeDtypeStruct((rows, 3 * cols), jnp.float32)]
    extra = [] if partial is None else [partial]
    if finish is not None:
        extra.extend(finish)
        held = [2] if joint else [1, 1]
        out_shape = [
            jax.ShapeDtypeStruct((rows, cols), jnp.float32),
            jax.ShapeDtypeStruct((2, rows), jnp.float32),
        ] + [jax.ShapeDtypeStruct((size, rows, cols), jnp.bfloat16) for size in held]
    return pl.pallas_call(
        functools.partial(
            project_kernel,
            parts,
            blocks,
            spots,
            partial is None,
            finish is not None,
            len(shards) + len(sources) + len(extra),
        ),
        in_specs=[pl.BlockSpec(memory_space=pltpu.SMEM), whole, whole]
        + [anywhere] * (len(shards) + len(sources))
        + [whole] * len(extra),
        out_specs=[whole] * len(out_shape),
        out_shape=out_shape,
        scratch_shapes=[
            pltpu.VMEM((rows, 3 * cols), jnp.float32),
            pltpu.VMEM((count, rows, feats), jnp.bfloat16),
            pltpu.VMEM((count, 3, feats, cols), jnp.bfloat16),
            pltpu.VMEM((2, rows, 2 * feats), jnp.bfloat16),
            pltpu.SemaphoreType.DMA((count, len(parts))),
            pltpu.SemaphoreType.DMA((count, 3)),
        ],
        compiler_params=pltpu.CompilerParams(vmem_limit_bytes=VMEM),
        cost_estimate=pl.CostEstimate(
            flops=6 * rows * count * feats * cols,
            bytes_accessed=2 * count * feats * (rows + 3 * cols) + 12 * rows * cols,
            transcendentals=0,
        ),
        name="project",
    )(place, stats, modulation, *shards, *sources, *extra)


def turn_kernel(count, width, squares_ref, gain_ref, *refs):
    for number in range(count):
        raw_ref, out_ref = refs[number], refs[4 * count + number]
        tables = [ref[...] for ref in refs[count + 3 * number : count + 3 * number + 3]]
        rows, cols = raw_ref.shape
        scale = lax.rsqrt(squares_ref[number : number + 1, :] * (1.0 / width) + epsilon)
        raw = raw_ref[...] * jnp.transpose(jnp.broadcast_to(scale, (128, rows)))[:, :1]
        for head in range(cols // HEAD_DIM):
            out_ref[:, head * HEAD_DIM : (head + 1) * HEAD_DIM] = turned(
                raw, gain_ref, tables, head
            ).astype(jnp.bfloat16)


def turn(raws, squares, gain, tables, width):
    count = len(raws)
    rows, cols = raws[0].shape
    whole = pl.BlockSpec(memory_space=pltpu.VMEM)
    return pl.pallas_call(
        functools.partial(turn_kernel, count, width),
        in_specs=[whole] * (2 + 4 * count),
        out_specs=[whole] * count,
        out_shape=[jax.ShapeDtypeStruct((rows, cols), jnp.bfloat16)] * count,
        compiler_params=pltpu.CompilerParams(vmem_limit_bytes=VMEM),
        cost_estimate=pl.CostEstimate(flops=0, bytes_accessed=0, transcendentals=0),
        name="turn",
    )(squares, gain, *raws, *[part for table in tables for part in table])


def attend_kernel(places, me_ref, bounds_ref, q_ref, *refs):
    count = len(places)
    pieces, (query_seg_ref, key_seg_ref, factor_ref) = refs[:count], refs[count : count + 3]
    out_ref, keys, values, highest, mixed, sems = refs[count + 3 :]
    me = me_ref[0]
    rows = pieces[0].shape[1]
    low, high = bounds_ref[0], bounds_ref[1]
    first = low * KEY_TILE // rows
    end = (high * KEY_TILE + rows - 1) // rows
    for number, (piece, (kind, at)) in enumerate(zip(pieces, places)):
        owner = me ^ (number % (count // 2))
        held = (keys, values)[kind]
        target = held.at[pl.ds(pl.multiple_of(owner * rows, rows), rows), :]
        sem = sems.at[kind, owner]

        @pl.when((owner >= first) & (owner < end))
        def _(source=piece.at[at], target=target, sem=sem):
            pltpu.make_async_copy(source, target, sem).start()

    def arrive(owner, carry):
        for kind, held in enumerate((keys, values)):
            target = held.at[pl.ds(pl.multiple_of(owner * rows, rows), rows), :]
            pltpu.make_async_copy(pieces[0].at[0], target, sems.at[kind, owner]).wait()
        return carry

    dim = HEAD_DIM
    heads = q_ref.shape[1] // dim
    ones = jnp.ones((KEY_TILE, dim), jnp.bfloat16)
    highest[...] = jnp.full_like(highest, -1e29)
    mixed[...] = jnp.zeros_like(mixed)
    query_seg = jnp.transpose(jnp.broadcast_to(query_seg_ref[...], (128, rows)))[:, :1]

    def step(block, carry):
        begin = jnp.where(block == low, first, (block * KEY_TILE + rows - 1) // rows)
        lax.fori_loop(begin, ((block + 1) * KEY_TILE + rows - 1) // rows, arrive, 0)
        where = pl.ds(pl.multiple_of(block * KEY_TILE, KEY_TILE), KEY_TILE)
        same = query_seg == key_seg_ref[block]
        factor = factor_ref[block]
        for head in range(heads):
            cols = slice(head * dim, (head + 1) * dim)
            scores = lax.dot_general(
                q_ref[:, cols],
                keys[where, cols],
                (((1,), (1,)), ((), ())),
                preferred_element_type=jnp.float32,
            )
            scores = jnp.where(same, scores * factor, -1e30)
            former = highest[head]
            newest = jnp.maximum(former, jnp.max(scores, axis=1, keepdims=True))
            highest[head] = newest
            weights = jnp.exp2(scores - newest[:, :1]).astype(jnp.bfloat16)
            right = jnp.concatenate([values[where, cols], ones], axis=1)
            part = jnp.dot(weights, right, preferred_element_type=jnp.float32)
            shrink = jnp.exp2(former - newest)
            mixed[head, :, :dim] = mixed[head, :, :dim] * shrink + part[:, :dim]
            mixed[head, :, dim:] = mixed[head, :, dim:] * shrink + part[:, dim:]
        return carry

    lax.fori_loop(low, high, step, 0)
    for head in range(heads):
        out_ref[:, head * dim : (head + 1) * dim] = (
            mixed[head, :, :dim] / mixed[head, :, dim:]
        ).astype(out_ref.dtype)


def key_bounds(query_seg, segment_ids):
    low = jnp.sum(segment_ids < query_seg[0], dtype=jnp.int32)
    high = jnp.sum(segment_ids <= query_seg[-1], dtype=jnp.int32)
    return jnp.stack([low // KEY_TILE, (high + KEY_TILE - 1) // KEY_TILE])


def attend(query, keys, values, me, bounds, query_seg, key_seg, factor):
    rows, cols = query.shape
    pieces = [array for array, _ in keys + values]
    places = tuple((0, at) for _, at in keys) + tuple((1, at) for _, at in values)
    count = len(pieces)
    tokens = key_seg.shape[0] * KEY_TILE
    dim = HEAD_DIM
    heads = cols // dim
    smem = pl.BlockSpec(memory_space=pltpu.SMEM)
    whole = pl.BlockSpec(memory_space=pltpu.VMEM)
    return pl.pallas_call(
        functools.partial(attend_kernel, places),
        in_specs=[smem, smem, whole] + [pl.BlockSpec(memory_space=pl.ANY)] * count + [whole] * 3,
        out_specs=whole,
        scratch_shapes=[
            pltpu.VMEM((tokens, cols), jnp.bfloat16),
            pltpu.VMEM((tokens, cols), jnp.bfloat16),
            pltpu.VMEM((heads, rows, dim), jnp.float32),
            pltpu.VMEM((heads, rows, 2 * dim), jnp.float32),
            pltpu.SemaphoreType.DMA((2, count // 2)),
        ],
        out_shape=jax.ShapeDtypeStruct((rows, cols), jnp.bfloat16),
        compiler_params=pltpu.CompilerParams(vmem_limit_bytes=VMEM),
        cost_estimate=pl.CostEstimate(
            flops=2 * rows * tokens * cols,
            bytes_accessed=4 * tokens * cols + 4 * rows * cols,
            transcendentals=rows * tokens * heads // 2,
        ),
        name="attend",
    )(me.reshape(1), bounds, query, *pieces, query_seg, key_seg, factor)


def pages_kernel(places, me_ref, page_ref, *refs):
    count = len(places)
    pieces, rest = refs[:count], refs[count:]
    scale_ref, (out_refs, held, sems) = (rest[0] if len(rest) == 5 else None), (
        rest[-4:-2],
        rest[-2],
        rest[-1],
    )
    me = me_ref[0]
    wanted = held.shape[0]
    per_block = pieces[0].shape[1] // PAGE
    waits = []
    for number in range(wanted):
        page = page_ref[number]
        rows = pl.ds(pl.multiple_of((page % per_block) * PAGE, PAGE), PAGE)
        target, sem = held.at[number], sems.at[number]
        for owner, (piece, at) in enumerate(zip(pieces, places)):

            @pl.when((page // per_block) == (me ^ owner))
            def _(source=piece.at[at, rows, :], target=target, sem=sem):
                pltpu.make_async_copy(source, target, sem).start()

        waits.append(pltpu.make_async_copy(pieces[0].at[0, pl.ds(0, PAGE), :], target, sem))
    for number in range(wanted):
        waits[number].wait()
        page = held[number]
        if scale_ref is not None:
            scale = jnp.broadcast_to(scale_ref[page_ref[number]], (128, PAGE))
            page = page.astype(jnp.float32) * jnp.transpose(scale)[:, :1]
        each = wanted // 2
        out_refs[number // each][number % each] = page.astype(jnp.bfloat16)


def pick_pages(pieces, me, pages, scale):
    _, rows, cols = pieces[0][0].shape
    wanted = pages.shape[0]
    smem = pl.BlockSpec(memory_space=pltpu.SMEM)
    whole = pl.BlockSpec(memory_space=pltpu.VMEM)
    extra = [] if scale is None else [scale]
    return pl.pallas_call(
        functools.partial(pages_kernel, tuple(at for _, at in pieces)),
        in_specs=[smem, smem]
        + [pl.BlockSpec(memory_space=pl.ANY)] * len(pieces)
        + [whole] * len(extra),
        out_specs=[whole] * 2,
        out_shape=[jax.ShapeDtypeStruct((wanted // 2, PAGE, cols), jnp.bfloat16)] * 2,
        scratch_shapes=[
            pltpu.VMEM((wanted, PAGE, cols), jnp.bfloat16),
            pltpu.SemaphoreType.DMA((wanted,)),
        ],
        compiler_params=pltpu.CompilerParams(vmem_limit_bytes=VMEM),
        cost_estimate=pl.CostEstimate(flops=0, bytes_accessed=0, transcendentals=0),
        name="pick_pages",
    )(me.reshape(1), pages, *[array for array, _ in pieces], *extra)


def own_pages(page_table, start, count):
    page_total = page_table.shape[0]
    inverse = (
        jnp.zeros((page_total,), jnp.int32)
        .at[page_table]
        .set(jnp.arange(page_total, dtype=jnp.int32))
    )
    return lax.dynamic_slice_in_dim(inverse, start, count, 0)


def whole_heads(ring, hidden, modulation, weights, gains, positions, segment_ids, page_table):
    tok_rows = hidden.shape[0]
    me = lax.axis_index("row")
    full_rows = lax.all_gather(hidden, "col", axis=1, tiled=True)
    modulated = modulate(full_rows.astype(jnp.float32), modulation)
    width = full_rows.shape[1]
    raws = [
        jnp.dot(
            modulated,
            lax.all_gather(weight, "row", axis=0, tiled=True),
            preferred_element_type=jnp.float32,
        )
        for weight in weights
    ]
    squares = lax.psum(tuple(jnp.sum(raw * raw, axis=1) for raw in raws[:2]), "col")
    tables = rotary_lanes(positions, HEAD_DIM)
    query, key = [
        turn([raw], total[None], gain[None], [tables], width)[0]
        for raw, total, gain in zip(raws, squares, gains)
    ]
    held = lax.all_gather(jnp.stack([key, raws[2].astype(jnp.bfloat16)]), "row", axis=0)
    keys, values = [[(held[number], kind) for number in range(ring)] for kind in range(2)]
    none = jnp.zeros((), jnp.int32)
    query_seg = lax.dynamic_slice_in_dim(segment_ids, me * tok_rows, tok_rows, 0)
    key_seg = segment_ids.astype(jnp.float32).reshape(-1, 1, KEY_TILE)
    attended = attend(
        query,
        keys,
        values,
        none,
        key_bounds(query_seg, segment_ids),
        query_seg.astype(jnp.float32)[None, :],
        key_seg,
        jnp.full_like(key_seg, HEAD_DIM ** (-0.5) * LOG2E),
    )
    count = tok_rows // PAGE
    pages = own_pages(page_table, me * count, count)
    pages = jnp.concatenate([pages, pages])
    picked = [pick_pages(pieces, none, pages, None)[0] for pieces in (keys, values)]
    return attended, jnp.stack(picked)


def split_heads(ring, ranks, hidden, modulation, weights, gains, positions, segment_ids, page_table):
    tok_rows, shard = hidden.shape
    width = ranks * shard
    me = lax.axis_index("row")
    rank = lax.axis_index("col")
    top = ring // 2
    half = me // top
    cols = weights[0].shape[1] // 2
    hops = []
    bit = top // 2
    while bit:
        hops.append(bit)
        bit //= 2

    def swap(value, bit):
        return lax.ppermute(value, "row", [(i, i ^ bit) for i in range(ring)])

    def across(value, step):
        return lax.ppermute(value, "col", [(c, c ^ step) for c in range(ranks)])

    def spread(blocks, bits):
        for bit in bits:
            blocks.update({number | bit: swap(blocks[number], bit) for number in list(blocks)})
        return blocks

    def in_order(mine, other, axis):
        return jnp.where(
            half == 0,
            jnp.concatenate([mine, other], axis=axis),
            jnp.concatenate([other, mine], axis=axis),
        )

    hidden_all = lax.all_gather(hidden, "col", axis=0)
    w_query, w_key, w_value = weights
    own, send_pair, send_single = cut((w_key, w_value, w_query), half)
    first, rest_hops = hops[0], hops[1:]
    pair, single = swap(send_pair, top), swap(send_single, top)
    next_own = swap(own, first)
    own_blocks = spread({0: own}, rest_hops)

    rows = hidden.astype(jnp.float32)
    local_mean = jnp.mean(rows, axis=1)
    local_square = jnp.sum(jnp.square(rows - local_mean[:, None]), axis=1)
    stats = jnp.stack([local_mean, local_square])
    all_stats = [stats] + [across(stats, step) for step in range(1, ranks)]
    average = sum(part[0] for part in all_stats) / ranks
    variance = (
        sum(part[1] + shard * jnp.square(part[0] - average) for part in all_stats) / width
    )
    small = jnp.concatenate(
        [jnp.stack([average, lax.rsqrt(variance + epsilon)]), positions.astype(jnp.float32)]
    )
    small_other = swap(small, top)
    moved = (pair, single, next_own, own_blocks, small, small_other)
    moved, hidden_late = lax.optimization_barrier((moved, hidden))
    pair, single, next_own, own_blocks, small, small_other = moved

    next_single = swap(single, first)
    other_rows = swap(hidden_late, top)
    pair_blocks = spread({0: pair}, rest_hops)
    single_blocks = spread({0: single}, rest_hops)
    next_own_blocks = spread({0: next_own}, rest_hops)
    early = tok_rows * 11 // 24 // 16 * 16
    sent = jnp.concatenate(
        [
            lax.dynamic_slice(hidden_all, (rank ^ step, early, 0), (1, tok_rows - early, shard))
            for step in range(1, ranks)
        ]
    ).reshape(-1, shard)
    moved = (next_single, other_rows, pair_blocks, single_blocks, next_own_blocks, sent)
    plain = (small, small_other, segment_ids, page_table, gains)
    moved, hidden_all, plain = lax.optimization_barrier((moved, hidden_all, plain))
    next_single, other_rows, pair_blocks, single_blocks, next_own_blocks, sent = moved
    small, small_other, segment_ids, page_table, gains = plain

    rest = swap(sent, top)
    next_pair = swap(pair_blocks[0], first)
    early_shards = [across(other_rows[:early], step) for step in range(1, ranks)]
    sources, spots = [], [None] * ring
    for number in own_blocks:
        for offset, whole in ((0, own_blocks), (first, next_own_blocks)):
            spots[number | offset] = tuple((len(sources), m) for m in range(3))
            sources.append(whole[number])
        at = len(sources)
        spots[number | top] = ((at, 0), (at, 1), (at + 1, 0))
        sources.extend([pair_blocks[number], single_blocks[number]])
    here = tuple(number for number in range(ring) if spots[number] is not None)
    late = tuple(number for number in range(ring) if spots[number] is None)
    own_parts = ((tok_rows, (0,), True),)
    place = jnp.stack([me, rank]).astype(jnp.int32)
    (partial,) = project(
        place,
        small[:2],
        modulation,
        own_parts,
        here,
        [hidden_all],
        tuple(spots),
        list(sources),
        None,
        None,
    )
    tables = [rotary_lanes(part[2:], HEAD_DIM) for part in (small, small_other)]
    q_gain, k_gain = [
        lax.dynamic_slice_in_dim(gain, half * cols, cols, 0)[None, :] for gain in gains
    ]
    count = tok_rows // PAGE
    pages = jnp.concatenate(
        [own_pages(page_table, owner * count, count) for owner in (me ^ top, me)]
    )
    query_segs = [
        lax.dynamic_slice_in_dim(segment_ids, owner * tok_rows, tok_rows, 0)
        for owner in (me, me ^ top)
    ]
    bounds = [key_bounds(seg, segment_ids) for seg in query_segs]
    query_segs = [seg.astype(jnp.float32)[None, :] for seg in query_segs]
    key_seg = segment_ids.astype(jnp.float32).reshape(-1, 1, KEY_TILE)
    prepared = (tables, q_gain, k_gain, pages, query_segs, key_seg, bounds)
    moved = (next_pair, next_single, rest, early_shards)
    moved, prepared, partial = lax.optimization_barrier((moved, prepared, partial))
    next_pair, next_single, rest, early_shards = moved
    tables, q_gain, k_gain, pages, query_segs, key_seg, bounds = prepared

    next_pair_blocks = spread({0: next_pair}, rest_hops)
    next_single_blocks = spread({0: next_single}, rest_hops)
    for number in own_blocks:
        at = len(sources)
        spots[number | top | first] = ((at, 0), (at, 1), (at + 1, 0))
        sources.extend([next_pair_blocks[number], next_single_blocks[number]])
    other_parts = (
        (early, (0,) * ranks, False),
        (
            tok_rows - early,
            (early,) + tuple(step * (tok_rows - early) for step in range(ranks - 1)),
            False,
        ),
    )
    late_sources = [part for number in own_blocks for part in (next_pair_blocks[number], next_single_blocks[number])]
    late_spots = list(spots)
    for at, number in enumerate(own_blocks):
        late_spots[number | top | first] = ((2 * at, 0), (2 * at, 1), (2 * at + 1, 0))
    own_query, own_squares, own_held = project(
        place,
        small[:2],
        modulation,
        own_parts,
        late,
        [hidden_all],
        tuple(late_spots),
        late_sources,
        partial,
        (k_gain, *tables[0]),
    )
    own_ahead = swap(own_held, first)
    other_query, other_squares, other_key, other_value = project(
        place,
        small_other[:2],
        modulation,
        other_parts,
        tuple(range(ring)),
        [other_rows] + early_shards + [other_rows] + [rest] * (ranks - 1),
        tuple(spots),
        sources,
        None,
        (k_gain, *tables[1]),
        joint=False,
    )
    value_ahead = swap(other_value, first)

    squares = jnp.stack([own_squares, other_squares])
    squares = squares + swap(squares, top)[::-1]
    bit = 1
    while bit < ranks:
        squares = squares + across(squares, bit)
        bit *= 2
    query = turn([own_query, other_query], squares[:, 1], q_gain, tables, width)
    key_squares = {0: squares[:, 0]}
    key_squares[first] = swap(key_squares[0], first)
    key_ahead = swap(other_key, first)
    key_squares[0], query, own_ahead, value_ahead = lax.optimization_barrier(
        (key_squares[0], query, own_ahead, value_ahead)
    )
    key_squares = spread(key_squares, rest_hops)
    blocks = jnp.stack([key_squares[n % top][n // top] for n in range(ring)])
    scale = lax.rsqrt(blocks / width + epsilon)
    scale = jnp.concatenate(
        [lax.dynamic_slice_in_dim(scale, me ^ owner, 1, 0) for owner in range(ring)]
    )
    factor = (scale * (HEAD_DIM ** (-0.5) * LOG2E)).reshape(-1, 1, KEY_TILE)
    scale = scale.reshape(-1, 1, PAGE)
    held = spread({0: own_held, first: own_ahead}, rest_hops)
    other_values = spread({0: other_value, first: value_ahead}, rest_hops)
    values = [(held[n], 1) for n in range(top)] + [(other_values[n], 0) for n in range(top)]
    values_picked = pick_pages(values, me, pages, None)
    key_ahead, values_picked = lax.optimization_barrier((key_ahead, values_picked))
    values_other = swap(values_picked[0], top)
    other_keys = spread({0: other_key, first: key_ahead}, rest_hops)
    keys = [(held[n], 0) for n in range(top)] + [(other_keys[n], 0) for n in range(top)]
    keys_picked = pick_pages(keys, me, pages, scale)
    query, keys_picked = lax.optimization_barrier((query, keys_picked))
    keys_other = swap(keys_picked[0], top)

    def attended(number):
        return attend(
            query[number], keys, values, me, bounds[number], query_segs[number], key_seg, factor
        )

    for_other = attended(1)
    query, for_other = lax.optimization_barrier((query, for_other))
    from_other = swap(for_other, top)
    for_me = attended(0)
    page_store = [
        in_order(keys_picked[1], keys_other, -1),
        in_order(values_picked[1], values_other, -1),
    ]
    return in_order(for_me, from_other, -1), jnp.stack(page_store)


def solution(mesh):
    ring, ranks = mesh.shape["row"], mesh.shape["col"]

    def body(
        hidden, modulation, w_query, w_key, w_value, q_gain, k_gain, positions, segment_ids, page_table
    ):
        rest = (
            hidden,
            modulation,
            (w_query, w_key, w_value),
            (q_gain, k_gain),
            positions,
            segment_ids,
            page_table,
        )
        heads = w_query.shape[1] // HEAD_DIM
        feats, shard = w_query.shape[0], hidden.shape[1]
        powers = ring & (ring - 1) == 0 and ranks & (ranks - 1) == 0
        if heads % 2 == 0 and ring >= 8 and powers and feats % 128 == 0 and shard % feats == 0:
            return split_heads(ring, ranks, *rest)
        return whole_heads(ring, *rest)

    in_specs = (
        P("row", "col"),
        P(),
        P("row", "col"),
        P("row", "col"),
        P("row", "col"),
        P("col"),
        P("col"),
        P(None, "row"),
        P(),
        P(),
    )
    out_specs = (P("row", "col"), P(None, "row", None, "col"))
    return jax.shard_map(body, mesh=mesh, in_specs=in_specs, out_specs=out_specs, check_vma=False)
```

profile of v0, /device:TPU:9, one launch (start us, length us, event | category | flops | bytes accessed | tf_op | source)
XLA Modules:
  0.0 249.9 jit_solution(5771377727146901652)
XLA Ops:
  7.2 0.7 all-gather.3.cloned.1.call-update
  7.9 4.8 %cut.1 = (bf16[3,640,640]{2,1,0:T(8,128)(2,1)}, bf16[2,640,640]{2,1,0:T(8,128)(2,1)}, bf16[1,640,640]{2,1,0:T(8,128)(2,1)}) custom-call(s32[1]{0:T(128)} %bitcast.1.half_ref, bf16[640,1280]{1,0:T(8,128)(2,1)} %refs_0_.1, bf16[640,1280]{1,0:T(8,128)(2,1)} %refs_1_.1, bf16[640,1280]{1,0:T(8,128)(2,1)} %refs_2_.1), custom_call_target="tpu_custom_call" | custom-call | bytes 9830400 | tf_op jit(solution)/shard_map/cut/pallas_call | solution.py:72
  12.7 1.3 collective-permute-start.2
  14.0 1.0 collective-permute-start.3
  14.9 1.2 collective-permute-start
  17.0 1.4 collective-permute-start.6
  18.4 1.6 collective-permute-done.6
  20.0 3.9 %collective-permute-start.5 = (f32[2,384]{1,0:T(2,128)S(1)}, f32[2,384]{1,0:T(2,128)S(1)}, u32[]{:S(2)}, u32[]{:S(2)}) collective-permute-start(f32[2,384]{1,0:T(2,128)S(1)} %pad_maximum_fusion.4), channel_id=1, source_target_pairs={{0,2},{1,3},{2,0},{3,1},{4,6},{5,7},{6,4},{7,5},{8,10},{9,11},{10,... | collective-permute-start | bytes 9224 | tf_op jit(solution)/shard_map/ppermute | solution.py:513
  23.8 1.4 collective-permute-done.5
  25.3 1.6 collective-permute-start.4
  26.8 1.4 collective-permute-done.4
  28.3 1.3 collective-permute-start.7
  29.6 40.8 %collective-permute-done.7 = f32[5,384]{1,0:T(8,128)S(1)} collective-permute-done((f32[5,384]{1,0:T(8,128)S(1)}, f32[5,384]{1,0:T(8,128)S(1)}, u32[]{:S(2)}, u32[]{:S(2)}) %collective-permute-start.7) | collective-permute-done | bytes 7712 | tf_op jit(solution)/shard_map/ppermute | solution.py:510
  70.4 0.9 copy-done.10
  71.3 0.8 collective-permute-start.12
  72.2 1.2 collective-permute-start.9
  73.7 1.0 collective-permute-start.11
  75.3 9.6 %all-gather.3.cloned.1.call-done = bf16[1536,1280]{1,0:T(8,128)(2,1)} async-done(((bf16[384,1280]{1,0:T(8,128)(2,1)}), bf16[1536,1280]{1,0:T(8,128)(2,1)}) %all-gather.3.cloned.1.call-update) | async-done | bytes 3932176 | tf_op jit(solution)/shard_map/all_gather | solution.py:527
  84.9 1.5 constant_dynamic-slice_fusion.10
  86.4 1.3 pad_maximum_fusion.1
  87.7 5.1 %collective-permute-done.8.refs_2_.refs_17_ = bf16[1,640,640]{2,1,0:T(8,128)(2,1)} collective-permute-done((bf16[1,640,640]{2,1,0:T(8,128)(2,1)}, bf16[1,640,640]{2,1,0:T(8,128)(2,1)}, u32[]{:S(2)}, u32[]{:S(2)}) %collective-permute-start.8) | collective-permute-done | bytes 819232 | tf_op jit(solution)/shard_map/ppermute | solution.py:510
  92.8 2.4 collective-permute-done.9.refs_0_.refs_4_
  95.2 1.8 slice.107
  97.2 2.3 collective-permute-start.16
  99.9 1.2 collective-permute-start.14
  101.2 0.7 fusion.22
  101.9 0.7 fusion.21
  102.6 3.9 %convert_reduce_fusion.2 = (s32[]{:T(128)}, s32[]{:T(128)}, s32[]{:T(128)}, s32[]{:T(128)}, f32[3072]{0:T(1024)}) fusion(s32[3072]{0:T(1024)S(1)} %copy-done.14, s32[]{:T(128)} %bitcast.9, s32[]{:T(128)} %bitcast.11, s32[]{:T(128)} %bitcast.7, s32[]{:T(128)} %bitcast.5), kind=kLoop, calls=%fused_computation.23 | loop fusion | flops 39932 | bytes 24608 | tf_op jit(solution)/shard_map/reduce_sum | solution.py:350
  116.1 0.6 scatter_custom_fusion
  117.5 0.7 pad_add_fusion.1
  118.2 2.6 %fusion.4 = (f32[384,128]{1,0:T(8,128)}, f32[384,128]{1,0:T(8,128)}, f32[384,128]{1,0:T(8,128)}, f32[384,128]{1,0:T(8,128)}, f32[384,128]{1,0:T(8,128)}, /*index=5*/f32[384,128]{1,0:T(8,128)}) fusion(f32[384]{0:T(512)S(1)} %get-tuple-element.157, f32[384]{0:T(512)S(1)} %get-tuple-element.158, f32[384]{0:T(512)S(1)} %get-tuple-element.156, ...), kind=kLoop, calls=%fused_computation.14 | loop fusion | flops 786432 | bytes 1190784 | tf_op jit(solution)/shard_map/jit(_where)/select_n | solution.py:38
  120.8 14.7 %project.3.refs_5_ = f32[384,1920]{1,0:T(8,128)} custom-call(s32[2]{0:T(128)} %pad_add_fusion.3.place_ref, f32[2,384]{1,0:T(2,128)} %slice.118.stats_ref, f32[2,5120]{1,0:T(2,128)} %modulation_ref.5, bf16[4,384,1280]{2,1,0:T(8,128)(2,1)} %bitcast.23, bf16[3,640,640]{2,1,0:T(8,128)(2,1)} %get-tuple-element.97.refs_1_.refs_8_, bf16[3,640,640]{2,1,0:T(8,128)(2,1)} %copy-done.4, ...), custom_call_target="tpu_custom_call" | custom-call | flops 5662310400 | bytes 20643840 | tf_op jit(solution)/shard_map/project/pallas_call | solution.py:223
  135.5 2.3 collective-permute-done.17.refs_3_
  137.9 2.5 collective-permute-start.18
  141.1 3.9 %collective-permute-done.19.refs_4_.refs_19_ = bf16[1,640,640]{2,1,0:T(8,128)(2,1)} collective-permute-done((bf16[1,640,640]{2,1,0:T(8,128)(2,1)}, bf16[1,640,640]{2,1,0:T(8,128)(2,1)}, u32[]{:S(2)}, u32[]{:S(2)}) %collective-permute-start.19) | collective-permute-done | bytes 819232 | tf_op jit(solution)/shard_map/ppermute | solution.py:510
  144.9 8.5 %project.4 = (f32[384,640]{1,0:T(8,128)}, f32[2,384]{1,0:T(2,128)}, bf16[2,384,640]{2,1,0:T(8,128)(2,1)}) custom-call(s32[2]{0:T(128)} %pad_add_fusion.3.place_ref, f32[2,384]{1,0:T(2,128)} %slice.118.stats_ref, f32[2,5120]{1,0:T(2,128)} %modulation_ref.5, bf16[4,384,1280]{2,1,0:T(8,128)(2,1)} %bitcast.24, bf16[2,640,640]{2,1,0:T(8,128)(2,1)} %copy-done.6, ...), custom_call_target="tpu_custom_call" | custom-call | flops 1887436800 | bytes 8847360 | tf_op jit(solution)/shard_map/project/pallas_call | solution.py:223
  153.8 15.9 %project.5 = (f32[384,640]{1,0:T(8,128)}, f32[2,384]{1,0:T(2,128)}, bf16[1,384,640]{2,1,0:T(8,128)(2,1)}, bf16[1,384,640]{2,1,0:T(8,128)(2,1)}) custom-call(s32[2]{0:T(128)} %pad_add_fusion.3.place_ref, f32[2,384]{1,0:T(2,128)} %slice.119.stats_ref, f32[2,5120]{1,0:T(2,128)} %modulation_ref.5, bf16[384,1280]{1,0:T(8,128)(2,1)} %collective-permute-done.9.refs_0_.refs_4_, ...), custom_call_target="tpu_custom_call" | custom-call | flops 7549747200 | bytes 26542080 | tf_op jit(solution)/shard_map/project/pallas_call | solution.py:223
  169.7 0.7 stack.62
  170.4 1.3 collective-permute-start.20
  171.7 1.3 collective-permute-start.24
  173.4 2.8 %collective-permute-done.21 = f32[2,2,384]{2,0,1:T(2,128)S(1)} collective-permute-done((f32[2,2,384]{2,0,1:T(2,128)S(1)}, f32[2,2,384]{2,0,1:T(2,128)S(1)}, u32[]{:S(2)}, u32[]{:S(2)}) %collective-permute-start.21) | collective-permute-done | bytes 6176 | tf_op jit(solution)/shard_map/ppermute | solution.py:513
  176.2 2.2 collective-permute-start.22
  178.4 2.6 %collective-permute-start.25 = (bf16[2,384,640]{2,1,0:T(8,128)(2,1)S(1)}, bf16[2,384,640]{2,1,0:T(8,128)(2,1)S(1)}, u32[]{:S(2)}, u32[]{:S(2)}) collective-permute-start(bf16[2,384,640]{2,1,0:T(8,128)(2,1)S(1)} %copy-done), channel_id=1, source_target_pairs={{0,4},{4,0},{8,12},{12,8},{16,20},{20,16},{24,28},{28,24},{1,5},{5... | collective-permute-start | bytes 2949128 | tf_op jit(solution)/shard_map/ppermute | solution.py:510
  181.6 4.0 %turn.1 = (bf16[384,640]{1,0:T(8,128)(2,1)}, bf16[384,640]{1,0:T(8,128)(2,1)}) custom-call(f32[2,384]{1,0:T(2,128)} %get-tuple-element.188.squares_ref, f32[1,640]{1,0:T(1,128)} %broadcast_in_dim.76.gain_ref, f32[384,640]{1,0:T(8,128)} %get-tuple-element.122.refs_0_, f32[384,640]{1,0:T(8,128)} %get-tuple-element.123.refs_1_, ...), custom_call_target="tpu_custom_call" | custom-call | tf_op jit(solution)/shard_map/turn/pallas_call | solution.py:273
  185.6 1.8 collective-permute-done.24.refs_6_.refs_14_
  187.4 1.1 collective-permute-start.26
  189.4 1.6 collective-permute-done.33
  191.0 1.2 collective-permute-start.34
  192.2 0.8 collective-permute-done.34
  193.5 0.6 collective-permute-start.30
  194.3 1.7 collective-permute-done.30.refs_7_.refs_15_
  196.0 3.0 %pick_pages.2 = (bf16[3,128,640]{2,1,0:T(8,128)(2,1)}, bf16[3,128,640]{2,1,0:T(8,128)(2,1)}) custom-call(s32[1]{0:T(128)} %bitcast.me_ref, s32[6]{0:T(128)} %pad_add_fusion.page_ref, bf16[2,384,640]{2,1,0:T(8,128)(2,1)} %get-tuple-element.126.refs_0_.refs_8_, bf16[2,384,640]{2,1,0:T(8,128)(2,1)} %copy-done.2, bf16[2,384,640]{2,1,0:T(8,128)(2,1)} %copy-done.1, ...), custom_call_target="tpu_custom_call" | custom-call | tf_op jit(solution)/shard_map/pick_pages/pallas_call | solution.py:426
  199.0 6.8 %collective-permute-done.28.refs_6_ = bf16[1,384,640]{2,1,0:T(8,128)(2,1)} collective-permute-done((bf16[1,384,640]{2,1,0:T(8,128)(2,1)}, bf16[1,384,640]{2,1,0:T(8,128)(2,1)}, u32[]{:S(2)}, u32[]{:S(2)}) %collective-permute-start.28) | collective-permute-done | bytes 491552 | tf_op jit(solution)/shard_map/ppermute | solution.py:510
  205.8 1.2 collective-permute-start.31
  207.1 0.6 reshape.211.refs_8_
  207.7 1.2 collective-permute-start.37
  209.5 0.8 copy-done.8
  210.3 0.8 copy-done.9
  211.1 3.5 %pick_pages.3 = (bf16[3,128,640]{2,1,0:T(8,128)(2,1)}, bf16[3,128,640]{2,1,0:T(8,128)(2,1)}) custom-call(s32[1]{0:T(128)} %bitcast.me_ref, s32[6]{0:T(128)} %pad_add_fusion.page_ref, bf16[2,384,640]{2,1,0:T(8,128)(2,1)} %get-tuple-element.126.refs_0_.refs_8_, bf16[2,384,640]{2,1,0:T(8,128)(2,1)} %copy-done.2, bf16[2,384,640]{2,1,0:T(8,128)(2,1)} %copy-done.1, ...), custom_call_target="tpu_custom_call" | custom-call | tf_op jit(solution)/shard_map/pick_pages/pallas_call | solution.py:426
  215.0 13.3 %attend.2 = bf16[384,640]{1,0:T(8,128)(2,1)} custom-call(s32[1]{0:T(128)} %bitcast.me_ref, s32[2]{0:T(128)} %get-tuple-element.142.bounds_ref, bf16[384,640]{1,0:T(8,128)(2,1)} %get-tuple-element.141.q_ref, bf16[2,384,640]{2,1,0:T(8,128)(2,1)} %get-tuple-element.126.refs_0_.refs_8_, bf16[2,384,640]{2,1,0:T(8,128)(2,1)} %copy-done.2, ...), custom_call_target="tpu_custom_call" | custom-call | flops 1509949440 | bytes 8847360 | tf_op jit(solution)/shard_map/attend/pallas_call | solution.py:365
  228.3 10.7 %attend.3 = bf16[384,640]{1,0:T(8,128)(2,1)} custom-call(s32[1]{0:T(128)} %bitcast.me_ref, s32[2]{0:T(128)} %get-tuple-element.104.bounds_ref, bf16[384,640]{1,0:T(8,128)(2,1)} %get-tuple-element.145.q_ref, bf16[2,384,640]{2,1,0:T(8,128)(2,1)} %get-tuple-element.126.refs_0_.refs_8_, bf16[2,384,640]{2,1,0:T(8,128)(2,1)} %copy-done.2, ...), custom_call_target="tpu_custom_call" | custom-call | flops 1509949440 | bytes 8847360 | tf_op jit(solution)/shard_map/attend/pallas_call | solution.py:365
  239.4 0.8 copy-done.13
  240.4 1.4 pad_maximum_fusion
  241.8 1.2 maximum_select_fusion
  (124 shorter events, 11.4 us)
Async XLA Ops:
  7.2 77.7 %all-gather.3.cloned.1.call-start = ((), (), s32[]{:S(2)}) async-start(), calls=%async_computation | async-start | bytes 4915200 | tf_op jit(solution)/shard_map/all_gather | solution.py:527
  7.9 8.5 %copy-start.5 = (bf16[384,1280]{1,0:T(8,128)(2,1)S(1)}, bf16[384,1280]{1,0:T(8,128)(2,1)}, u32[]{:S(2)}) copy-start(bf16[384,1280]{1,0:T(8,128)(2,1)} %param.10) | copy-start | bytes 2949124
  12.7 14.1 %copy-start.15 = (s32[3,384]{1,0:T(4,128)S(1)}, s32[3,384]{1,0:T(4,128)}, u32[]{:S(2)}) copy-start(s32[3,384]{1,0:T(4,128)} %param.17) | copy-start | bytes 13828
  12.7 57.7 %collective-permute-start.2 = (bf16[3,640,640]{2,1,0:T(8,128)(2,1)}, bf16[3,640,640]{2,1,0:T(8,128)(2,1)S(1)}, u32[]{:S(2)}, u32[]{:S(2)}) collective-permute-start(bf16[3,640,640]{2,1,0:T(8,128)(2,1)} %get-tuple-element.97.refs_1_.refs_8_), channel_id=1, source_target_pairs={{0,8},{4,12},{8,0},{12,4},{16,24},{20,28},{24,16},{28,20},{1,9},{5... | collective-permute-start | bytes 7372808 | tf_op jit(solution)/shard_map/ppermute | solution.py:510
  14.0 57.4 %collective-permute-start.3 = (bf16[3,640,640]{2,1,0:T(8,128)(2,1)}, bf16[3,640,640]{2,1,0:T(8,128)(2,1)}, u32[]{:S(2)}, u32[]{:S(2)}) collective-permute-start(bf16[3,640,640]{2,1,0:T(8,128)(2,1)} %get-tuple-element.97.refs_1_.refs_8_), channel_id=1, source_target_pairs={{0,4},{4,0},{8,12},{12,8},{16,20},{20,16},{24,28},{28,24},{1,5},{5... | collective-permute-start | bytes 7372808 | tf_op jit(solution)/shard_map/ppermute | solution.py:510
  14.9 55.5 %collective-permute-start = (bf16[2,640,640]{2,1,0:T(8,128)(2,1)}, bf16[2,640,640]{2,1,0:T(8,128)(2,1)}, u32[]{:S(2)}, u32[]{:S(2)}) collective-permute-start(bf16[2,640,640]{2,1,0:T(8,128)(2,1)} %get-tuple-element.77), channel_id=1, source_target_pairs={{0,16},{4,20},{8,24},{12,28},{16,0},{20,4},{24,8},{28,12},{1,17},{... | collective-permute-start | bytes 4915208 | tf_op jit(solution)/shard_map/ppermute | solution.py:510
  16.2 54.2 %collective-permute-start.1 = (bf16[1,640,640]{2,1,0:T(8,128)(2,1)}, bf16[1,640,640]{2,1,0:T(8,128)(2,1)S(1)}, u32[]{:S(2)}, u32[]{:S(2)}) collective-permute-start(bf16[1,640,640]{2,1,0:T(8,128)(2,1)} %get-tuple-element.78), channel_id=1, source_target_pairs={{0,16},{4,20},{8,24},{12,28},{16,0},{20,4},{24,8},{28,12},{1,17},{... | collective-permute-start | bytes 2457608 | tf_op jit(solution)/shard_map/ppermute | solution.py:510
  17.0 2.9 %collective-permute-start.6 = (f32[2,384]{1,0:T(2,128)S(1)}, f32[2,384]{1,0:T(2,128)S(1)}, u32[]{:S(2)}, u32[]{:S(2)}) collective-permute-start(f32[2,384]{1,0:T(2,128)S(1)} %pad_maximum_fusion.4), channel_id=1, source_target_pairs={{0,3},{1,2},{2,1},{3,0},{4,7},{5,6},{6,5},{7,4},{8,11},{9,10},{10,... | collective-permute-start | bytes 9224 | tf_op jit(solution)/shard_map/ppermute | solution.py:513
  20.0 5.3 %collective-permute-start.5 = (f32[2,384]{1,0:T(2,128)S(1)}, f32[2,384]{1,0:T(2,128)S(1)}, u32[]{:S(2)}, u32[]{:S(2)}) collective-permute-start(f32[2,384]{1,0:T(2,128)S(1)} %pad_maximum_fusion.4), channel_id=1, source_target_pairs={{0,2},{1,3},{2,0},{3,1},{4,6},{5,7},{6,4},{7,5},{8,10},{9,11},{10,... | collective-permute-start | bytes 9224 | tf_op jit(solution)/shard_map/ppermute | solution.py:513
  25.3 3.0 %collective-permute-start.4 = (f32[2,384]{1,0:T(2,128)S(1)}, f32[2,384]{1,0:T(2,128)S(1)}, u32[]{:S(2)}, u32[]{:S(2)}) collective-permute-start(f32[2,384]{1,0:T(2,128)S(1)} %pad_maximum_fusion.4), channel_id=1, source_target_pairs={{0,1},{1,0},{2,3},{3,2},{4,5},{5,4},{6,7},{7,6},{8,9},{9,8},{10,11... | collective-permute-start | bytes 9224 | tf_op jit(solution)/shard_map/ppermute | solution.py:513
  28.3 42.1 %collective-permute-start.7 = (f32[5,384]{1,0:T(8,128)S(1)}, f32[5,384]{1,0:T(8,128)S(1)}, u32[]{:S(2)}, u32[]{:S(2)}) collective-permute-start(f32[5,384]{1,0:T(8,128)S(1)} %pad_maximum_fusion.2), channel_id=1, source_target_pairs={{0,16},{4,20},{8,24},{12,28},{16,0},{20,4},{24,8},{28,12},{1,17},{... | collective-permute-start | bytes 23048 | tf_op jit(solution)/shard_map/ppermute | solution.py:510
  70.4 0.9 copy-start.10
  71.3 16.4 %copy-start.4 = (bf16[3,640,640]{2,1,0:T(8,128)(2,1)}, bf16[3,640,640]{2,1,0:T(8,128)(2,1)S(1)}, u32[]{:S(2)}) copy-start(bf16[3,640,640]{2,1,0:T(8,128)(2,1)S(1)} %collective-permute-done.2.refs_2_.refs_9_) | copy-start | bytes 7372804
  71.3 23.9 %collective-permute-start.12 = (bf16[3,640,640]{2,1,0:T(8,128)(2,1)S(1)}, bf16[3,640,640]{2,1,0:T(8,128)(2,1)}, u32[]{:S(2)}, u32[]{:S(2)}) collective-permute-start(bf16[3,640,640]{2,1,0:T(8,128)(2,1)S(1)} %collective-permute-done.2.refs_2_.refs_9_), channel_id=1, source_target_pairs={{0,4},{4,0},{8,12},{12,8},{16,20},{20,16},{24,28},{28,24},{1,5},{5... | collective-permute-start | bytes 7372808 | tf_op jit(solution)/shard_map/ppermute | solution.py:510
  72.1 23.1 %collective-permute-start.10 = (bf16[2,640,640]{2,1,0:T(8,128)(2,1)}, bf16[2,640,640]{2,1,0:T(8,128)(2,1)}, u32[]{:S(2)}, u32[]{:S(2)}) collective-permute-start(bf16[2,640,640]{2,1,0:T(8,128)(2,1)} %collective-permute-done.refs_3_.refs_10_), channel_id=1, source_target_pairs={{0,4},{4,0},{8,12},{12,8},{16,20},{20,16},{24,28},{28,24},{1,5},{5... | collective-permute-start | bytes 4915208 | tf_op jit(solution)/shard_map/ppermute | solution.py:510
  72.2 23.0 %collective-permute-start.9 = (bf16[384,1280]{1,0:T(8,128)(2,1)S(1)}, bf16[384,1280]{1,0:T(8,128)(2,1)}, u32[]{:S(2)}, u32[]{:S(2)}) collective-permute-start(bf16[384,1280]{1,0:T(8,128)(2,1)S(1)} %copy-done.5), channel_id=1, source_target_pairs={{0,16},{4,20},{8,24},{12,28},{16,0},{20,4},{24,8},{28,12},{1,17},{... | collective-permute-start | bytes 2949128 | tf_op jit(solution)/shard_map/ppermute | solution.py:510
  73.4 19.4 %collective-permute-start.8 = (bf16[1,640,640]{2,1,0:T(8,128)(2,1)}, bf16[1,640,640]{2,1,0:T(8,128)(2,1)}, u32[]{:S(2)}, u32[]{:S(2)}) collective-permute-start(bf16[1,640,640]{2,1,0:T(8,128)(2,1)} %copy-done.10), channel_id=1, source_target_pairs={{0,8},{4,12},{8,0},{12,4},{16,24},{20,28},{24,16},{28,20},{1,9},{5... | collective-permute-start | bytes 2457608 | tf_op jit(solution)/shard_map/ppermute | solution.py:510
  73.7 19.1 %collective-permute-start.11 = (bf16[1,640,640]{2,1,0:T(8,128)(2,1)}, bf16[1,640,640]{2,1,0:T(8,128)(2,1)}, u32[]{:S(2)}, u32[]{:S(2)}) collective-permute-start(bf16[1,640,640]{2,1,0:T(8,128)(2,1)} %copy-done.10), channel_id=1, source_target_pairs={{0,4},{4,0},{8,12},{12,8},{16,20},{20,16},{24,28},{28,24},{1,5},{5... | collective-permute-start | bytes 2457608 | tf_op jit(solution)/shard_map/ppermute | solution.py:510
  86.3 14.8 %copy-start.14 = (s32[3072]{0:T(1024)S(1)}, s32[3072]{0:T(1024)}, u32[]{:S(2)}) copy-start(s32[3072]{0:T(1024)} %param.18) | copy-start | bytes 36868
  86.4 26.7 %copy-start.17 = (f32[1280]{0:T(1024)S(1)}, f32[1280]{0:T(1024)}, u32[]{:S(2)}) copy-start(f32[1280]{0:T(1024)} %param.15) | copy-start | bytes 15364
  86.4 27.4 %copy-start.18 = (f32[1280]{0:T(1024)S(1)}, f32[1280]{0:T(1024)}, u32[]{:S(2)}) copy-start(f32[1280]{0:T(1024)} %param.16) | copy-start | bytes 15364
  86.4 29.7 %copy-start.19 = (s32[24]{0:T(128)S(1)}, s32[24]{0:T(128)}, u32[]{:S(2)}) copy-start(s32[24]{0:T(128)} %param.19) | copy-start | bytes 292
  97.0 38.5 %collective-permute-start.15 = (bf16[176,1280]{1,0:T(8,128)(2,1)}, bf16[176,1280]{1,0:T(8,128)(2,1)}, u32[]{:S(2)}, u32[]{:S(2)}) collective-permute-start(bf16[176,1280]{1,0:T(8,128)(2,1)} %slice.107), channel_id=1, source_target_pairs={{0,1},{1,0},{2,3},{3,2},{4,5},{5,4},{6,7},{7,6},{8,9},{9,8},{10,11... | collective-permute-start | bytes 1351688 | tf_op jit(solution)/shard_map/ppermute | solution.py:513
  97.2 38.3 %collective-permute-start.16 = (bf16[176,1280]{1,0:T(8,128)(2,1)}, bf16[176,1280]{1,0:T(8,128)(2,1)}, u32[]{:S(2)}, u32[]{:S(2)}) collective-permute-start(bf16[176,1280]{1,0:T(8,128)(2,1)} %slice.107), channel_id=1, source_target_pairs={{0,2},{1,3},{2,0},{3,1},{4,6},{5,7},{6,4},{7,5},{8,10},{9,11},{10,... | collective-permute-start | bytes 1351688 | tf_op jit(solution)/shard_map/ppermute | solution.py:513
  99.5 38.4 %collective-permute-start.17 = (bf16[176,1280]{1,0:T(8,128)(2,1)}, bf16[176,1280]{1,0:T(8,128)(2,1)}, u32[]{:S(2)}, u32[]{:S(2)}) collective-permute-start(bf16[176,1280]{1,0:T(8,128)(2,1)} %slice.107), channel_id=1, source_target_pairs={{0,3},{1,2},{2,1},{3,0},{4,7},{5,6},{6,5},{7,4},{8,11},{9,10},{10,... | collective-permute-start | bytes 1351688 | tf_op jit(solution)/shard_map/ppermute | solution.py:513
  99.7 38.2 %collective-permute-start.13 = (bf16[2,640,640]{2,1,0:T(8,128)(2,1)}, bf16[2,640,640]{2,1,0:T(8,128)(2,1)S(1)}, u32[]{:S(2)}, u32[]{:S(2)}) collective-permute-start(bf16[2,640,640]{2,1,0:T(8,128)(2,1)} %collective-permute-done.refs_3_.refs_10_), channel_id=1, source_target_pairs={{0,8},{4,12},{8,0},{12,4},{16,24},{20,28},{24,16},{28,20},{1,9},{5... | collective-permute-start | bytes 4915208 | tf_op jit(solution)/shard_map/ppermute | solution.py:510
  99.9 38.0 %collective-permute-start.14 = (bf16[624,1280]{1,0:T(8,128)(2,1)}, bf16[624,1280]{1,0:T(8,128)(2,1)S(1)}, u32[]{:S(2)}, u32[]{:S(2)}) collective-permute-start(bf16[624,1280]{1,0:T(8,128)(2,1)} %bitcast.3), channel_id=1, source_target_pairs={{0,16},{4,20},{8,24},{12,28},{16,0},{20,4},{24,8},{28,12},{1,17},{... | collective-permute-start | bytes 4792328 | tf_op jit(solution)/shard_map/ppermute | solution.py:510
  137.9 15.5 %copy-start.3 = (bf16[624,1280]{1,0:T(8,128)(2,1)}, bf16[624,1280]{1,0:T(8,128)(2,1)S(1)}, u32[]{:S(2)}) copy-start(bf16[624,1280]{1,0:T(8,128)(2,1)S(1)} %collective-permute-done.14.refs_5_.refs_6_.refs_7_) | copy-start | bytes 4792324
  137.9 7.0 %copy-start.6 = (bf16[2,640,640]{2,1,0:T(8,128)(2,1)}, bf16[2,640,640]{2,1,0:T(8,128)(2,1)S(1)}, u32[]{:S(2)}) copy-start(bf16[2,640,640]{2,1,0:T(8,128)(2,1)S(1)} %collective-permute-done.13.refs_1_.refs_16_) | copy-start | bytes 4915204
  137.9 7.0 %collective-permute-start.18 = (bf16[2,640,640]{2,1,0:T(8,128)(2,1)S(1)}, bf16[2,640,640]{2,1,0:T(8,128)(2,1)}, u32[]{:S(2)}, u32[]{:S(2)}) collective-permute-start(bf16[2,640,640]{2,1,0:T(8,128)(2,1)S(1)} %collective-permute-done.13.refs_1_.refs_16_), channel_id=1, source_target_pairs={{0,4},{4,0},{8,12},{12,8},{16,20},{20,16},{24,28},{28,24},{1,5},{5... | collective-permute-start | bytes 4915208 | tf_op jit(solution)/shard_map/ppermute | solution.py:510
  140.4 4.5 %collective-permute-start.19 = (bf16[1,640,640]{2,1,0:T(8,128)(2,1)}, bf16[1,640,640]{2,1,0:T(8,128)(2,1)}, u32[]{:S(2)}, u32[]{:S(2)}) collective-permute-start(bf16[1,640,640]{2,1,0:T(8,128)(2,1)} %collective-permute-done.8.refs_2_.refs_17_), channel_id=1, source_target_pairs={{0,4},{4,0},{8,12},{12,8},{16,20},{20,16},{24,28},{28,24},{1,5},{5... | collective-permute-start | bytes 2457608 | tf_op jit(solution)/shard_map/ppermute | solution.py:510
  153.4 17.0 %copy-start.16 = (f32[2,384]{1,0:T(2,128)S(1)}, f32[2,384]{1,0:T(2,128)}, u32[]{:S(2)}) copy-start(f32[2,384]{1,0:T(2,128)} %get-tuple-element.112) | copy-start | bytes 9220
  153.4 25.0 %copy-start = (bf16[2,384,640]{2,1,0:T(8,128)(2,1)S(1)}, bf16[2,384,640]{2,1,0:T(8,128)(2,1)}, u32[]{:S(2)}) copy-start(bf16[2,384,640]{2,1,0:T(8,128)(2,1)} %get-tuple-element.126.refs_0_.refs_8_) | copy-start | bytes 2949124
  153.5 34.0 %collective-permute-start.23 = (bf16[2,384,640]{2,1,0:T(8,128)(2,1)}, bf16[2,384,640]{2,1,0:T(8,128)(2,1)S(1)}, u32[]{:S(2)}, u32[]{:S(2)}) collective-permute-start(bf16[2,384,640]{2,1,0:T(8,128)(2,1)} %get-tuple-element.126.refs_0_.refs_8_), channel_id=1, source_target_pairs={{0,8},{4,12},{8,0},{12,4},{16,24},{20,28},{24,16},{28,20},{1,9},{5... | collective-permute-start | bytes 2949128 | tf_op jit(solution)/shard_map/ppermute | solution.py:510
  169.6 19.4 %copy-start.7 = (bf16[1,384,640]{2,1,0:T(8,128)(2,1)S(1)}, bf16[1,384,640]{2,1,0:T(8,128)(2,1)}, u32[]{:S(2)}) copy-start(bf16[1,384,640]{2,1,0:T(8,128)(2,1)} %get-tuple-element.127.refs_4_.refs_12_) | copy-start | bytes 1474564
  170.4 2.8 %collective-permute-start.20 = (f32[2,2,384]{2,0,1:T(2,128)S(1)}, f32[2,2,384]{2,0,1:T(2,128)S(1)}, u32[]{:S(2)}, u32[]{:S(2)}) collective-permute-start(f32[2,2,384]{2,0,1:T(2,128)S(1)} %pad_maximum_fusion.3), channel_id=1, source_target_pairs={{0,16},{4,20},{8,24},{12,28},{16,0},{20,4},{24,8},{28,12},{1,17},{... | collective-permute-start | bytes 18440 | tf_op jit(solution)/shard_map/ppermute | solution.py:510
  171.7 15.7 %collective-permute-start.24 = (bf16[1,384,640]{2,1,0:T(8,128)(2,1)}, bf16[1,384,640]{2,1,0:T(8,128)(2,1)}, u32[]{:S(2)}, u32[]{:S(2)}) collective-permute-start(bf16[1,384,640]{2,1,0:T(8,128)(2,1)} %get-tuple-element.127.refs_4_.refs_12_), channel_id=1, source_target_pairs={{0,8},{4,12},{8,0},{12,4},{16,24},{20,28},{24,16},{28,20},{1,9},{5... | collective-permute-start | bytes 1474568 | tf_op jit(solution)/shard_map/ppermute | solution.py:510
  173.4 2.8 %collective-permute-start.21 = (f32[2,2,384]{2,0,1:T(2,128)S(1)}, f32[2,2,384]{2,0,1:T(2,128)S(1)}, u32[]{:S(2)}, u32[]{:S(2)}) collective-permute-start(f32[2,2,384]{2,0,1:T(2,128)S(1)} %fusion.14), channel_id=1, source_target_pairs={{0,1},{1,0},{2,3},{3,2},{4,5},{5,4},{6,7},{7,6},{8,9},{9,8},{10,11... | collective-permute-start | bytes 18440 | tf_op jit(solution)/shard_map/ppermute | solution.py:513
  176.2 4.8 %collective-permute-start.22 = (f32[2,2,384]{2,0,1:T(2,128)S(1)}, f32[2,2,384]{2,0,1:T(2,128)S(1)}, u32[]{:S(2)}, u32[]{:S(2)}) collective-permute-start(f32[2,2,384]{2,0,1:T(2,128)S(1)} %fusion.24), channel_id=1, source_target_pairs={{0,2},{1,3},{2,0},{3,1},{4,6},{5,7},{6,4},{7,5},{8,10},{9,11},{10,... | collective-permute-start | bytes 18440 | tf_op jit(solution)/shard_map/ppermute | solution.py:513
  178.4 15.9 %collective-permute-start.25 = (bf16[2,384,640]{2,1,0:T(8,128)(2,1)S(1)}, bf16[2,384,640]{2,1,0:T(8,128)(2,1)S(1)}, u32[]{:S(2)}, u32[]{:S(2)}) collective-permute-start(bf16[2,384,640]{2,1,0:T(8,128)(2,1)S(1)} %copy-done), channel_id=1, source_target_pairs={{0,4},{4,0},{8,12},{12,8},{16,20},{20,16},{24,28},{28,24},{1,5},{5... | collective-permute-start | bytes 2949128 | tf_op jit(solution)/shard_map/ppermute | solution.py:510
  187.4 8.6 %copy-start.1 = (bf16[2,384,640]{2,1,0:T(8,128)(2,1)}, bf16[2,384,640]{2,1,0:T(8,128)(2,1)S(1)}, u32[]{:S(2)}) copy-start(bf16[2,384,640]{2,1,0:T(8,128)(2,1)S(1)} %collective-permute-done.23.refs_2_.refs_10_) | copy-start | bytes 2949124
  187.4 8.6 %collective-permute-start.26 = (bf16[2,384,640]{2,1,0:T(8,128)(2,1)S(1)}, bf16[2,384,640]{2,1,0:T(8,128)(2,1)}, u32[]{:S(2)}, u32[]{:S(2)}) collective-permute-start(bf16[2,384,640]{2,1,0:T(8,128)(2,1)S(1)} %collective-permute-done.23.refs_2_.refs_10_), channel_id=1, source_target_pairs={{0,4},{4,0},{8,12},{12,8},{16,20},{20,16},{24,28},{28,24},{1,5},{5... | collective-permute-start | bytes 2949128 | tf_op jit(solution)/shard_map/ppermute | solution.py:510
  188.5 2.4 collective-permute-start.33
  189.0 5.2 %collective-permute-start.29 = (bf16[1,384,640]{2,1,0:T(8,128)(2,1)S(1)}, bf16[1,384,640]{2,1,0:T(8,128)(2,1)}, u32[]{:S(2)}, u32[]{:S(2)}) collective-permute-start(bf16[1,384,640]{2,1,0:T(8,128)(2,1)S(1)} %copy-done.7), channel_id=1, source_target_pairs={{0,4},{4,0},{8,12},{12,8},{16,20},{20,16},{24,28},{28,24},{1,5},{5... | collective-permute-start | bytes 1474568 | tf_op jit(solution)/shard_map/ppermute | solution.py:510
  191.0 2.0 collective-permute-start.34
  192.2 1.3 collective-permute-start.32
  193.0 12.8 %collective-permute-start.28 = (bf16[1,384,640]{2,1,0:T(8,128)(2,1)}, bf16[1,384,640]{2,1,0:T(8,128)(2,1)}, u32[]{:S(2)}, u32[]{:S(2)}) collective-permute-start(bf16[1,384,640]{2,1,0:T(8,128)(2,1)} %get-tuple-element.132.refs_4_), channel_id=1, source_target_pairs={{0,8},{4,12},{8,0},{12,4},{16,24},{20,28},{24,16},{28,20},{1,9},{5... | collective-permute-start | bytes 1474568 | tf_op jit(solution)/shard_map/ppermute | solution.py:510
  193.5 2.5 collective-permute-start.30
  194.2 15.3 %collective-permute-start.27 = (bf16[1,384,640]{2,1,0:T(8,128)(2,1)}, bf16[1,384,640]{2,1,0:T(8,128)(2,1)S(1)}, u32[]{:S(2)}, u32[]{:S(2)}) collective-permute-start(bf16[1,384,640]{2,1,0:T(8,128)(2,1)} %get-tuple-element.132.refs_4_), channel_id=1, source_target_pairs={{0,4},{4,0},{8,12},{12,8},{16,20},{20,16},{24,28},{28,24},{1,5},{5... | collective-permute-start | bytes 1474568 | tf_op jit(solution)/shard_map/ppermute | solution.py:510
  194.3 1.7 copy-start.2
  205.8 3.7 %collective-permute-start.31 = (bf16[1,384,640]{2,1,0:T(8,128)(2,1)}, bf16[1,384,640]{2,1,0:T(8,128)(2,1)S(1)}, u32[]{:S(2)}, u32[]{:S(2)}) collective-permute-start(bf16[1,384,640]{2,1,0:T(8,128)(2,1)} %collective-permute-done.28.refs_6_), channel_id=1, source_target_pairs={{0,4},{4,0},{8,12},{12,8},{16,20},{20,16},{24,28},{28,24},{1,5},{5... | collective-permute-start | bytes 1474568 | tf_op jit(solution)/shard_map/ppermute | solution.py:510
  207.7 31.4 %collective-permute-start.37 = (bf16[3,128,640]{2,1,0:T(8,128)(2,1)}, bf16[3,128,640]{2,1,0:T(8,128)(2,1)S(1)}, u32[]{:S(2)}, u32[]{:S(2)}) collective-permute-start(bf16[3,128,640]{2,1,0:T(8,128)(2,1)} %get-tuple-element.151), channel_id=1, source_target_pairs={{0,16},{4,20},{8,24},{12,28},{16,0},{20,4},{24,8},{28,12},{1,17},{... | collective-permute-start | bytes 1474568 | tf_op jit(solution)/shard_map/ppermute | solution.py:510
  209.5 0.8 copy-start.8
  210.3 0.8 copy-start.9
  214.7 24.7 %collective-permute-start.36 = (bf16[3,128,640]{2,1,0:T(8,128)(2,1)}, bf16[3,128,640]{2,1,0:T(8,128)(2,1)S(1)}, u32[]{:S(2)}, u32[]{:S(2)}) collective-permute-start(bf16[3,128,640]{2,1,0:T(8,128)(2,1)} %get-tuple-element.149), channel_id=1, source_target_pairs={{0,16},{4,20},{8,24},{12,28},{16,0},{20,4},{24,8},{28,12},{1,17},{... | collective-permute-start | bytes 1474568 | tf_op jit(solution)/shard_map/ppermute | solution.py:510
  228.3 10.9 %copy-start.12 = (bf16[3,128,640]{2,1,0:T(8,128)(2,1)S(1)}, bf16[3,128,640]{2,1,0:T(8,128)(2,1)}, u32[]{:S(2)}) copy-start(bf16[3,128,640]{2,1,0:T(8,128)(2,1)} %get-tuple-element.150) | copy-start | bytes 1474564
  228.3 13.6 %collective-permute-start.35 = (bf16[384,640]{1,0:T(8,128)(2,1)}, bf16[384,640]{1,0:T(8,128)(2,1)S(1)}, u32[]{:S(2)}, u32[]{:S(2)}) collective-permute-start(bf16[384,640]{1,0:T(8,128)(2,1)} %attend.2), channel_id=1, source_target_pairs={{0,16},{4,20},{8,24},{12,28},{16,0},{20,4},{24,8},{28,12},{1,17},{... | collective-permute-start | bytes 1474568 | tf_op jit(solution)/shard_map/ppermute | solution.py:510
  239.1 1.0 copy-start.13
  240.4 1.5 copy-start.11
Sparse Core Ops, SparseCore 0:
  9.6 75.2 all-gather.2
where the time goes:
time: 253 us; the launch traced here: 250 us
  waiting for transfers between devices  84.9 us (34%)
  Pallas kernels  78.4 us (31%)
  starting transfers between devices  36.7 us (15%)
  between operations  21.1 us (8%)
  local copies, waits for them, and re-layouts  15.1 us (6%)
  other arithmetic  13.7 us (5%)
    ppermute x30, waiting for transfers between devices, swap(): return lax.ppermute(value, 'row', [(i, i ^ bit) for i in range(ring)])  65.2 us
    pallas_call x3, Pallas kernels, project(): pl.pallas_call(functools.partial(project_kernel, parts, blocks, spots, pa...  39 us
    ppermute x30, starting transfers between devices, swap(): return lax.ppermute(value, 'row', [(i, i ^ bit) for i in range(ring)])  25 us
    pallas_call x2, Pallas kernels, attend(): pl.pallas_call(functools.partial(attend_kernel, places), in_specs=[smem,...  24 us
    ppermute x8, starting transfers between devices, across(): return lax.ppermute(value, 'col', [(c, c ^ step) for c in range(ranks)])  11.7 us
    all_gather x1, waiting for transfers between devices, split_heads(): hidden_all = lax.all_gather(hidden, 'col', axis=0)  9.57 us
    ppermute x8, waiting for transfers between devices, across(): return lax.ppermute(value, 'col', [(c, c ^ step) for c in range(ranks)])  9.48 us
    pallas_call x2, Pallas kernels, pick_pages(): pl.pallas_call(functools.partial(pages_kernel, tuple((at for _, at in pie...  6.52 us
  transfers between devices with their start and end apart: 39, of which 16 were waited for; matrix products, arithmetic and copies ran while one was open for 9% of the time, Pallas kernels for 28%

commit v1 on v0

--- a/solution.py
+++ b/solution.py
@@ -259,10 +259,11 @@
         tables = [ref[...] for ref in refs[count + 3 * number : count + 3 * number + 3]]
         rows, cols = raw_ref.shape
         scale = lax.rsqrt(squares_ref[number : number + 1, :] * (1.0 / width) + epsilon)
-        raw = raw_ref[...] * jnp.transpose(jnp.broadcast_to(scale, (128, rows)))[:, :1]
+        scale = jnp.transpose(jnp.broadcast_to(scale, (HEAD_DIM, rows)))
         for head in range(cols // HEAD_DIM):
-            out_ref[:, head * HEAD_DIM : (head + 1) * HEAD_DIM] = turned(
-                raw, gain_ref, tables, head
+            lanes = slice(head * HEAD_DIM, (head + 1) * HEAD_DIM)
+            out_ref[:, lanes] = turned(
+                raw_ref[:, lanes] * scale, gain_ref[:, lanes], tables, 0
             ).astype(jnp.bfloat16)
 
 
@@ -311,13 +312,14 @@
     ones = jnp.ones((KEY_TILE, dim), jnp.bfloat16)
     highest[...] = jnp.full_like(highest, -1e29)
     mixed[...] = jnp.zeros_like(mixed)
-    query_seg = jnp.transpose(jnp.broadcast_to(query_seg_ref[...], (128, rows)))[:, :1]
+    query_seg = jnp.transpose(jnp.broadcast_to(query_seg_ref[...], (dim, rows)))
+    times = KEY_TILE // dim
 
     def step(block, carry):
         begin = jnp.where(block == low, first, (block * KEY_TILE + rows - 1) // rows)
         lax.fori_loop(begin, ((block + 1) * KEY_TILE + rows - 1) // rows, arrive, 0)
         where = pl.ds(pl.multiple_of(block * KEY_TILE, KEY_TILE), KEY_TILE)
-        same = query_seg == key_seg_ref[block]
+        same = jnp.concatenate([query_seg] * times, axis=1) == key_seg_ref[block]
         factor = factor_ref[block]
         for head in range(heads):
             cols = slice(head * dim, (head + 1) * dim)
@@ -331,7 +333,8 @@
             former = highest[head]
             newest = jnp.maximum(former, jnp.max(scores, axis=1, keepdims=True))
             highest[head] = newest
-            weights = jnp.exp2(scores - newest[:, :1]).astype(jnp.bfloat16)
+            weights = jnp.exp2(scores - jnp.concatenate([newest] * times, axis=1))
+            weights = weights.astype(jnp.bfloat16)
             right = jnp.concatenate([values[where, cols], ones], axis=1)
             part = jnp.dot(weights, right, preferred_element_type=jnp.float32)
             shrink = jnp.exp2(former - newest)
@@ -409,12 +412,16 @@
         waits.append(pltpu.make_async_copy(pieces[0].at[0, pl.ds(0, PAGE), :], target, sem))
     for number in range(wanted):
         waits[number].wait()
-        page = held[number]
-        if scale_ref is not None:
-            scale = jnp.broadcast_to(scale_ref[page_ref[number]], (128, PAGE))
-            page = page.astype(jnp.float32) * jnp.transpose(scale)[:, :1]
         each = wanted // 2
-        out_refs[number // each][number % each] = page.astype(jnp.bfloat16)
+        out_ref = out_refs[number // each].at[number % each]
+        if scale_ref is None:
+            out_ref[...] = held[number]
+            continue
+        scale = jnp.transpose(jnp.broadcast_to(scale_ref[page_ref[number]], (HEAD_DIM, PAGE)))
+        for start in range(0, held.shape[2], HEAD_DIM):
+            lanes = slice(start, start + HEAD_DIM)
+            page = held[number, :, lanes].astype(jnp.float32) * scale
+            out_ref[:, lanes] = page.astype(jnp.bfloat16)
 
 
 def pick_pages(pieces, me, pages, scale):

time: 253 us -> 253 us (level)
  no operation moved by 1% of the time
where the time goes in v1:
time: 253 us; the launch traced here: 252 us
  waiting for transfers between devices  85.5 us (34%)
  Pallas kernels  79.2 us (31%)
  starting transfers between devices  37.9 us (15%)
  between operations  21.1 us (8%)
  local copies, waits for them, and re-layouts  15.1 us (6%)
  other arithmetic  13.7 us (5%)
    ppermute x30, waiting for transfers between devices, swap(): return lax.ppermute(value, 'row', [(i, i ^ bit) for i in range(ring)])  65.7 us
    pallas_call x3, Pallas kernels, project(): pl.pallas_call(functools.partial(project_kernel, parts, blocks, spots, pa...  39 us
    ppermute x30, starting transfers between devices, swap(): return lax.ppermute(value, 'row', [(i, i ^ bit) for i in range(ring)])  26.1 us
    pallas_call x2, Pallas kernels, attend(): pl.pallas_call(functools.partial(attend_kernel, places), in_specs=[smem,...  25.3 us
    ppermute x8, starting transfers between devices, across(): return lax.ppermute(value, 'col', [(c, c ^ step) for c in range(ranks)])  11.7 us
    all_gather x1, waiting for transfers between devices, split_heads(): hidden_all = lax.all_gather(hidden, 'col', axis=0)  9.57 us
    ppermute x8, waiting for transfers between devices, across(): return lax.ppermute(value, 'col', [(c, c ^ step) for c in range(ranks)])  9.48 us
    pallas_call x2, Pallas kernels, pick_pages(): pl.pallas_call(functools.partial(pages_kernel, tuple((at for _, at in pie...  6.18 us
  transfers between devices with their start and end apart: 39, of which 16 were waited for; matrix products, arithmetic and copies ran while one was open for 9% of the time, Pallas kernels for 28%

profile of v1, /device:TPU:9, one launch (start us, length us, event | category | flops | bytes accessed | tf_op | source)
XLA Modules:
  0.0 252.4 jit_solution(14144311524838967505)
XLA Ops:
  7.2 0.7 all-gather.3.cloned.1.call-update
  7.9 4.8 %cut.1 = (bf16[3,640,640]{2,1,0:T(8,128)(2,1)}, bf16[2,640,640]{2,1,0:T(8,128)(2,1)}, bf16[1,640,640]{2,1,0:T(8,128)(2,1)}) custom-call(s32[1]{0:T(128)} %bitcast.1.half_ref, bf16[640,1280]{1,0:T(8,128)(2,1)} %refs_0_.1, bf16[640,1280]{1,0:T(8,128)(2,1)} %refs_1_.1, bf16[640,1280]{1,0:T(8,128)(2,1)} %refs_2_.1), custom_call_target="tpu_custom_call" | custom-call | bytes 9830400 | tf_op jit(solution)/shard_map/cut/pallas_call | solution.py:72
  12.7 1.3 collective-permute-start.2
  14.0 1.0 collective-permute-start.3
  14.9 1.2 collective-permute-start
  17.0 1.4 collective-permute-start.6
  18.4 1.6 collective-permute-done.6
  20.0 3.9 %collective-permute-start.5 = (f32[2,384]{1,0:T(2,128)S(1)}, f32[2,384]{1,0:T(2,128)S(1)}, u32[]{:S(2)}, u32[]{:S(2)}) collective-permute-start(f32[2,384]{1,0:T(2,128)S(1)} %pad_maximum_fusion.4), channel_id=1, source_target_pairs={{0,2},{1,3},{2,0},{3,1},{4,6},{5,7},{6,4},{7,5},{8,10},{9,11},{10,... | collective-permute-start | bytes 9224 | tf_op jit(solution)/shard_map/ppermute | solution.py:520
  23.8 1.4 collective-permute-done.5
  25.3 1.6 collective-permute-start.4
  26.8 1.4 collective-permute-done.4
  28.3 1.3 collective-permute-start.7
  29.6 40.8 %collective-permute-done.7 = f32[5,384]{1,0:T(8,128)S(1)} collective-permute-done((f32[5,384]{1,0:T(8,128)S(1)}, f32[5,384]{1,0:T(8,128)S(1)}, u32[]{:S(2)}, u32[]{:S(2)}) %collective-permute-start.7) | collective-permute-done | bytes 7712 | tf_op jit(solution)/shard_map/ppermute | solution.py:517
  70.4 0.9 copy-done.10
  71.3 0.8 collective-permute-start.12
  72.2 1.2 collective-permute-start.9
  73.7 1.0 collective-permute-start.11
  75.3 9.6 %all-gather.3.cloned.1.call-done = bf16[1536,1280]{1,0:T(8,128)(2,1)} async-done(((bf16[384,1280]{1,0:T(8,128)(2,1)}), bf16[1536,1280]{1,0:T(8,128)(2,1)}) %all-gather.3.cloned.1.call-update) | async-done | bytes 3932176 | tf_op jit(solution)/shard_map/all_gather | solution.py:534
  84.9 1.5 constant_dynamic-slice_fusion.10
  86.4 1.3 pad_maximum_fusion.1
  87.7 5.1 %collective-permute-done.8.refs_2_.refs_17_ = bf16[1,640,640]{2,1,0:T(8,128)(2,1)} collective-permute-done((bf16[1,640,640]{2,1,0:T(8,128)(2,1)}, bf16[1,640,640]{2,1,0:T(8,128)(2,1)}, u32[]{:S(2)}, u32[]{:S(2)}) %collective-permute-start.8) | collective-permute-done | bytes 819232 | tf_op jit(solution)/shard_map/ppermute | solution.py:517
  92.8 2.4 collective-permute-done.9.refs_0_.refs_4_
  95.2 1.8 slice.107
  97.2 2.3 collective-permute-start.16
  99.9 1.2 collective-permute-start.14
  101.2 0.7 fusion.22
  101.9 0.7 fusion.21
  102.6 3.9 %convert_reduce_fusion.2 = (s32[]{:T(128)}, s32[]{:T(128)}, s32[]{:T(128)}, s32[]{:T(128)}, f32[3072]{0:T(1024)}) fusion(s32[3072]{0:T(1024)S(1)} %copy-done.14, s32[]{:T(128)} %bitcast.9, s32[]{:T(128)} %bitcast.11, s32[]{:T(128)} %bitcast.7, s32[]{:T(128)} %bitcast.5), kind=kLoop, calls=%fused_computation.23 | loop fusion | flops 39932 | bytes 24608 | tf_op jit(solution)/shard_map/reduce_sum | solution.py:353
  116.1 0.6 scatter_custom_fusion
  117.5 0.7 pad_add_fusion.1
  118.2 2.6 %fusion.4 = (f32[384,128]{1,0:T(8,128)}, f32[384,128]{1,0:T(8,128)}, f32[384,128]{1,0:T(8,128)}, f32[384,128]{1,0:T(8,128)}, f32[384,128]{1,0:T(8,128)}, /*index=5*/f32[384,128]{1,0:T(8,128)}) fusion(f32[384]{0:T(512)S(1)} %get-tuple-element.157, f32[384]{0:T(512)S(1)} %get-tuple-element.158, f32[384]{0:T(512)S(1)} %get-tuple-element.156, ...), kind=kLoop, calls=%fused_computation.14 | loop fusion | flops 786432 | bytes 1190784 | tf_op jit(solution)/shard_map/jit(_where)/select_n | solution.py:38
  120.8 14.7 %project.3.refs_5_ = f32[384,1920]{1,0:T(8,128)} custom-call(s32[2]{0:T(128)} %pad_add_fusion.3.place_ref, f32[2,384]{1,0:T(2,128)} %slice.118.stats_ref, f32[2,5120]{1,0:T(2,128)} %modulation_ref.5, bf16[4,384,1280]{2,1,0:T(8,128)(2,1)} %bitcast.23, bf16[3,640,640]{2,1,0:T(8,128)(2,1)} %get-tuple-element.97.refs_1_.refs_8_, bf16[3,640,640]{2,1,0:T(8,128)(2,1)} %copy-done.4, ...), custom_call_target="tpu_custom_call" | custom-call | flops 5662310400 | bytes 20643840 | tf_op jit(solution)/shard_map/project/pallas_call | solution.py:223
  135.5 2.3 collective-permute-done.17.refs_3_
  137.9 2.5 collective-permute-start.18
  141.1 3.9 %collective-permute-done.19.refs_4_.refs_19_ = bf16[1,640,640]{2,1,0:T(8,128)(2,1)} collective-permute-done((bf16[1,640,640]{2,1,0:T(8,128)(2,1)}, bf16[1,640,640]{2,1,0:T(8,128)(2,1)}, u32[]{:S(2)}, u32[]{:S(2)}) %collective-permute-start.19) | collective-permute-done | bytes 819232 | tf_op jit(solution)/shard_map/ppermute | solution.py:517
  144.9 8.5 %project.4 = (f32[384,640]{1,0:T(8,128)}, f32[2,384]{1,0:T(2,128)}, bf16[2,384,640]{2,1,0:T(8,128)(2,1)}) custom-call(s32[2]{0:T(128)} %pad_add_fusion.3.place_ref, f32[2,384]{1,0:T(2,128)} %slice.118.stats_ref, f32[2,5120]{1,0:T(2,128)} %modulation_ref.5, bf16[4,384,1280]{2,1,0:T(8,128)(2,1)} %bitcast.24, bf16[2,640,640]{2,1,0:T(8,128)(2,1)} %copy-done.6, ...), custom_call_target="tpu_custom_call" | custom-call | flops 1887436800 | bytes 8847360 | tf_op jit(solution)/shard_map/project/pallas_call | solution.py:223
  153.8 15.9 %project.5 = (f32[384,640]{1,0:T(8,128)}, f32[2,384]{1,0:T(2,128)}, bf16[1,384,640]{2,1,0:T(8,128)(2,1)}, bf16[1,384,640]{2,1,0:T(8,128)(2,1)}) custom-call(s32[2]{0:T(128)} %pad_add_fusion.3.place_ref, f32[2,384]{1,0:T(2,128)} %slice.119.stats_ref, f32[2,5120]{1,0:T(2,128)} %modulation_ref.5, bf16[384,1280]{1,0:T(8,128)(2,1)} %collective-permute-done.9.refs_0_.refs_4_, ...), custom_call_target="tpu_custom_call" | custom-call | flops 7549747200 | bytes 26542080 | tf_op jit(solution)/shard_map/project/pallas_call | solution.py:223
  169.7 0.7 stack.62
  170.4 1.3 collective-permute-start.20
  171.7 1.3 collective-permute-start.24
  173.4 2.8 %collective-permute-done.21 = f32[2,2,384]{2,0,1:T(2,128)S(1)} collective-permute-done((f32[2,2,384]{2,0,1:T(2,128)S(1)}, f32[2,2,384]{2,0,1:T(2,128)S(1)}, u32[]{:S(2)}, u32[]{:S(2)}) %collective-permute-start.21) | collective-permute-done | bytes 6176 | tf_op jit(solution)/shard_map/ppermute | solution.py:520
  176.2 2.2 collective-permute-start.22
  178.4 2.6 %collective-permute-start.25 = (bf16[2,384,640]{2,1,0:T(8,128)(2,1)S(1)}, bf16[2,384,640]{2,1,0:T(8,128)(2,1)S(1)}, u32[]{:S(2)}, u32[]{:S(2)}) collective-permute-start(bf16[2,384,640]{2,1,0:T(8,128)(2,1)S(1)} %copy-done), channel_id=1, source_target_pairs={{0,4},{4,0},{8,12},{12,8},{16,20},{20,16},{24,28},{28,24},{1,5},{5... | collective-permute-start | bytes 2949128 | tf_op jit(solution)/shard_map/ppermute | solution.py:517
  181.6 3.9 %turn.1 = (bf16[384,640]{1,0:T(8,128)(2,1)}, bf16[384,640]{1,0:T(8,128)(2,1)}) custom-call(f32[2,384]{1,0:T(2,128)} %get-tuple-element.188.squares_ref, f32[1,640]{1,0:T(1,128)} %broadcast_in_dim.76.gain_ref, f32[384,640]{1,0:T(8,128)} %get-tuple-element.122.refs_0_, f32[384,640]{1,0:T(8,128)} %get-tuple-element.123.refs_1_, ...), custom_call_target="tpu_custom_call" | custom-call | tf_op jit(solution)/shard_map/turn/pallas_call | solution.py:274
  185.4 2.0 collective-permute-done.24.refs_6_.refs_14_
  187.4 1.1 collective-permute-start.26
  189.2 1.8 collective-permute-done.33
  191.0 1.2 collective-permute-start.34
  192.2 0.8 collective-permute-done.34
  194.1 1.7 collective-permute-done.30.refs_7_.refs_15_
  195.8 3.0 %pick_pages.2 = (bf16[3,128,640]{2,1,0:T(8,128)(2,1)}, bf16[3,128,640]{2,1,0:T(8,128)(2,1)}) custom-call(s32[1]{0:T(128)} %bitcast.me_ref, s32[6]{0:T(128)} %pad_add_fusion.page_ref, bf16[2,384,640]{2,1,0:T(8,128)(2,1)} %get-tuple-element.126.refs_0_.refs_8_, bf16[2,384,640]{2,1,0:T(8,128)(2,1)} %copy-done.2, bf16[2,384,640]{2,1,0:T(8,128)(2,1)} %copy-done.1, ...), custom_call_target="tpu_custom_call" | custom-call | tf_op jit(solution)/shard_map/pick_pages/pallas_call | solution.py:433
  198.8 7.0 %collective-permute-done.28.refs_6_ = bf16[1,384,640]{2,1,0:T(8,128)(2,1)} collective-permute-done((bf16[1,384,640]{2,1,0:T(8,128)(2,1)}, bf16[1,384,640]{2,1,0:T(8,128)(2,1)}, u32[]{:S(2)}, u32[]{:S(2)}) %collective-permute-start.28) | collective-permute-done | bytes 491552 | tf_op jit(solution)/shard_map/ppermute | solution.py:517
  205.8 1.2 collective-permute-start.31
  207.1 0.6 reshape.211.refs_8_
  207.7 1.2 collective-permute-start.37
  209.5 0.8 copy-done.8
  210.3 0.8 copy-done.9
  211.1 3.2 %pick_pages.3 = (bf16[3,128,640]{2,1,0:T(8,128)(2,1)}, bf16[3,128,640]{2,1,0:T(8,128)(2,1)}) custom-call(s32[1]{0:T(128)} %bitcast.me_ref, s32[6]{0:T(128)} %pad_add_fusion.page_ref, bf16[2,384,640]{2,1,0:T(8,128)(2,1)} %get-tuple-element.126.refs_0_.refs_8_, bf16[2,384,640]{2,1,0:T(8,128)(2,1)} %copy-done.2, bf16[2,384,640]{2,1,0:T(8,128)(2,1)} %copy-done.1, ...), custom_call_target="tpu_custom_call" | custom-call | tf_op jit(solution)/shard_map/pick_pages/pallas_call | solution.py:433
  214.6 12.7 %attend.2 = bf16[384,640]{1,0:T(8,128)(2,1)} custom-call(s32[1]{0:T(128)} %bitcast.me_ref, s32[2]{0:T(128)} %get-tuple-element.142.bounds_ref, bf16[384,640]{1,0:T(8,128)(2,1)} %get-tuple-element.141.q_ref, bf16[2,384,640]{2,1,0:T(8,128)(2,1)} %get-tuple-element.126.refs_0_.refs_8_, bf16[2,384,640]{2,1,0:T(8,128)(2,1)} %copy-done.2, ...), custom_call_target="tpu_custom_call" | custom-call | flops 1509949440 | bytes 8847360 | tf_op jit(solution)/shard_map/attend/pallas_call | solution.py:368
  227.4 1.6 collective-permute-start.35
  229.0 12.6 %attend.3 = bf16[384,640]{1,0:T(8,128)(2,1)} custom-call(s32[1]{0:T(128)} %bitcast.me_ref, s32[2]{0:T(128)} %get-tuple-element.104.bounds_ref, bf16[384,640]{1,0:T(8,128)(2,1)} %get-tuple-element.145.q_ref, bf16[2,384,640]{2,1,0:T(8,128)(2,1)} %get-tuple-element.126.refs_0_.refs_8_, bf16[2,384,640]{2,1,0:T(8,128)(2,1)} %copy-done.2, ...), custom_call_target="tpu_custom_call" | custom-call | flops 1509949440 | bytes 8847360 | tf_op jit(solution)/shard_map/attend/pallas_call | solution.py:368
  241.9 0.8 copy-done.13
  242.9 1.4 pad_maximum_fusion
  244.3 1.2 maximum_select_fusion
  (124 shorter events, 11.6 us)
Async XLA Ops:
  7.2 77.7 %all-gather.3.cloned.1.call-start = ((), (), s32[]{:S(2)}) async-start(), calls=%async_computation | async-start | bytes 4915200 | tf_op jit(solution)/shard_map/all_gather | solution.py:534
  7.9 8.5 %copy-start.5 = (bf16[384,1280]{1,0:T(8,128)(2,1)S(1)}, bf16[384,1280]{1,0:T(8,128)(2,1)}, u32[]{:S(2)}) copy-start(bf16[384,1280]{1,0:T(8,128)(2,1)} %param.10) | copy-start | bytes 2949124
  12.7 14.1 %copy-start.15 = (s32[3,384]{1,0:T(4,128)S(1)}, s32[3,384]{1,0:T(4,128)}, u32[]{:S(2)}) copy-start(s32[3,384]{1,0:T(4,128)} %param.17) | copy-start | bytes 13828
  12.7 57.7 %collective-permute-start.2 = (bf16[3,640,640]{2,1,0:T(8,128)(2,1)}, bf16[3,640,640]{2,1,0:T(8,128)(2,1)S(1)}, u32[]{:S(2)}, u32[]{:S(2)}) collective-permute-start(bf16[3,640,640]{2,1,0:T(8,128)(2,1)} %get-tuple-element.97.refs_1_.refs_8_), channel_id=1, source_target_pairs={{0,8},{4,12},{8,0},{12,4},{16,24},{20,28},{24,16},{28,20},{1,9},{5... | collective-permute-start | bytes 7372808 | tf_op jit(solution)/shard_map/ppermute | solution.py:517
  14.0 57.4 %collective-permute-start.3 = (bf16[3,640,640]{2,1,0:T(8,128)(2,1)}, bf16[3,640,640]{2,1,0:T(8,128)(2,1)}, u32[]{:S(2)}, u32[]{:S(2)}) collective-permute-start(bf16[3,640,640]{2,1,0:T(8,128)(2,1)} %get-tuple-element.97.refs_1_.refs_8_), channel_id=1, source_target_pairs={{0,4},{4,0},{8,12},{12,8},{16,20},{20,16},{24,28},{28,24},{1,5},{5... | collective-permute-start | bytes 7372808 | tf_op jit(solution)/shard_map/ppermute | solution.py:517
  14.9 55.5 %collective-permute-start = (bf16[2,640,640]{2,1,0:T(8,128)(2,1)}, bf16[2,640,640]{2,1,0:T(8,128)(2,1)}, u32[]{:S(2)}, u32[]{:S(2)}) collective-permute-start(bf16[2,640,640]{2,1,0:T(8,128)(2,1)} %get-tuple-element.77), channel_id=1, source_target_pairs={{0,16},{4,20},{8,24},{12,28},{16,0},{20,4},{24,8},{28,12},{1,17},{... | collective-permute-start | bytes 4915208 | tf_op jit(solution)/shard_map/ppermute | solution.py:517
  16.2 54.2 %collective-permute-start.1 = (bf16[1,640,640]{2,1,0:T(8,128)(2,1)}, bf16[1,640,640]{2,1,0:T(8,128)(2,1)S(1)}, u32[]{:S(2)}, u32[]{:S(2)}) collective-permute-start(bf16[1,640,640]{2,1,0:T(8,128)(2,1)} %get-tuple-element.78), channel_id=1, source_target_pairs={{0,16},{4,20},{8,24},{12,28},{16,0},{20,4},{24,8},{28,12},{1,17},{... | collective-permute-start | bytes 2457608 | tf_op jit(solution)/shard_map/ppermute | solution.py:517
  17.0 2.9 %collective-permute-start.6 = (f32[2,384]{1,0:T(2,128)S(1)}, f32[2,384]{1,0:T(2,128)S(1)}, u32[]{:S(2)}, u32[]{:S(2)}) collective-permute-start(f32[2,384]{1,0:T(2,128)S(1)} %pad_maximum_fusion.4), channel_id=1, source_target_pairs={{0,3},{1,2},{2,1},{3,0},{4,7},{5,6},{6,5},{7,4},{8,11},{9,10},{10,... | collective-permute-start | bytes 9224 | tf_op jit(solution)/shard_map/ppermute | solution.py:520
  20.0 5.3 %collective-permute-start.5 = (f32[2,384]{1,0:T(2,128)S(1)}, f32[2,384]{1,0:T(2,128)S(1)}, u32[]{:S(2)}, u32[]{:S(2)}) collective-permute-start(f32[2,384]{1,0:T(2,128)S(1)} %pad_maximum_fusion.4), channel_id=1, source_target_pairs={{0,2},{1,3},{2,0},{3,1},{4,6},{5,7},{6,4},{7,5},{8,10},{9,11},{10,... | collective-permute-start | bytes 9224 | tf_op jit(solution)/shard_map/ppermute | solution.py:520
  25.3 3.0 %collective-permute-start.4 = (f32[2,384]{1,0:T(2,128)S(1)}, f32[2,384]{1,0:T(2,128)S(1)}, u32[]{:S(2)}, u32[]{:S(2)}) collective-permute-start(f32[2,384]{1,0:T(2,128)S(1)} %pad_maximum_fusion.4), channel_id=1, source_target_pairs={{0,1},{1,0},{2,3},{3,2},{4,5},{5,4},{6,7},{7,6},{8,9},{9,8},{10,11... | collective-permute-start | bytes 9224 | tf_op jit(solution)/shard_map/ppermute | solution.py:520
  28.3 42.1 %collective-permute-start.7 = (f32[5,384]{1,0:T(8,128)S(1)}, f32[5,384]{1,0:T(8,128)S(1)}, u32[]{:S(2)}, u32[]{:S(2)}) collective-permute-start(f32[5,384]{1,0:T(8,128)S(1)} %pad_maximum_fusion.2), channel_id=1, source_target_pairs={{0,16},{4,20},{8,24},{12,28},{16,0},{20,4},{24,8},{28,12},{1,17},{... | collective-permute-start | bytes 23048 | tf_op jit(solution)/shard_map/ppermute | solution.py:517
  70.4 0.9 copy-start.10
  71.3 16.4 %copy-start.4 = (bf16[3,640,640]{2,1,0:T(8,128)(2,1)}, bf16[3,640,640]{2,1,0:T(8,128)(2,1)S(1)}, u32[]{:S(2)}) copy-start(bf16[3,640,640]{2,1,0:T(8,128)(2,1)S(1)} %collective-permute-done.2.refs_2_.refs_9_) | copy-start | bytes 7372804
  71.3 23.9 %collective-permute-start.12 = (bf16[3,640,640]{2,1,0:T(8,128)(2,1)S(1)}, bf16[3,640,640]{2,1,0:T(8,128)(2,1)}, u32[]{:S(2)}, u32[]{:S(2)}) collective-permute-start(bf16[3,640,640]{2,1,0:T(8,128)(2,1)S(1)} %collective-permute-done.2.refs_2_.refs_9_), channel_id=1, source_target_pairs={{0,4},{4,0},{8,12},{12,8},{16,20},{20,16},{24,28},{28,24},{1,5},{5... | collective-permute-start | bytes 7372808 | tf_op jit(solution)/shard_map/ppermute | solution.py:517
  72.1 23.1 %collective-permute-start.10 = (bf16[2,640,640]{2,1,0:T(8,128)(2,1)}, bf16[2,640,640]{2,1,0:T(8,128)(2,1)}, u32[]{:S(2)}, u32[]{:S(2)}) collective-permute-start(bf16[2,640,640]{2,1,0:T(8,128)(2,1)} %collective-permute-done.refs_3_.refs_10_), channel_id=1, source_target_pairs={{0,4},{4,0},{8,12},{12,8},{16,20},{20,16},{24,28},{28,24},{1,5},{5... | collective-permute-start | bytes 4915208 | tf_op jit(solution)/shard_map/ppermute | solution.py:517
  72.2 23.0 %collective-permute-start.9 = (bf16[384,1280]{1,0:T(8,128)(2,1)S(1)}, bf16[384,1280]{1,0:T(8,128)(2,1)}, u32[]{:S(2)}, u32[]{:S(2)}) collective-permute-start(bf16[384,1280]{1,0:T(8,128)(2,1)S(1)} %copy-done.5), channel_id=1, source_target_pairs={{0,16},{4,20},{8,24},{12,28},{16,0},{20,4},{24,8},{28,12},{1,17},{... | collective-permute-start | bytes 2949128 | tf_op jit(solution)/shard_map/ppermute | solution.py:517
  73.4 19.4 %collective-permute-start.8 = (bf16[1,640,640]{2,1,0:T(8,128)(2,1)}, bf16[1,640,640]{2,1,0:T(8,128)(2,1)}, u32[]{:S(2)}, u32[]{:S(2)}) collective-permute-start(bf16[1,640,640]{2,1,0:T(8,128)(2,1)} %copy-done.10), channel_id=1, source_target_pairs={{0,8},{4,12},{8,0},{12,4},{16,24},{20,28},{24,16},{28,20},{1,9},{5... | collective-permute-start | bytes 2457608 | tf_op jit(solution)/shard_map/ppermute | solution.py:517
  73.7 19.1 %collective-permute-start.11 = (bf16[1,640,640]{2,1,0:T(8,128)(2,1)}, bf16[1,640,640]{2,1,0:T(8,128)(2,1)}, u32[]{:S(2)}, u32[]{:S(2)}) collective-permute-start(bf16[1,640,640]{2,1,0:T(8,128)(2,1)} %copy-done.10), channel_id=1, source_target_pairs={{0,4},{4,0},{8,12},{12,8},{16,20},{20,16},{24,28},{28,24},{1,5},{5... | collective-permute-start | bytes 2457608 | tf_op jit(solution)/shard_map/ppermute | solution.py:517
  86.3 14.8 %copy-start.14 = (s32[3072]{0:T(1024)S(1)}, s32[3072]{0:T(1024)}, u32[]{:S(2)}) copy-start(s32[3072]{0:T(1024)} %param.18) | copy-start | bytes 36868
  86.4 26.7 %copy-start.17 = (f32[1280]{0:T(1024)S(1)}, f32[1280]{0:T(1024)}, u32[]{:S(2)}) copy-start(f32[1280]{0:T(1024)} %param.15) | copy-start | bytes 15364
  86.4 27.4 %copy-start.18 = (f32[1280]{0:T(1024)S(1)}, f32[1280]{0:T(1024)}, u32[]{:S(2)}) copy-start(f32[1280]{0:T(1024)} %param.16) | copy-start | bytes 15364
  86.4 29.7 %copy-start.19 = (s32[24]{0:T(128)S(1)}, s32[24]{0:T(128)}, u32[]{:S(2)}) copy-start(s32[24]{0:T(128)} %param.19) | copy-start | bytes 292
  97.0 38.5 %collective-permute-start.15 = (bf16[176,1280]{1,0:T(8,128)(2,1)}, bf16[176,1280]{1,0:T(8,128)(2,1)}, u32[]{:S(2)}, u32[]{:S(2)}) collective-permute-start(bf16[176,1280]{1,0:T(8,128)(2,1)} %slice.107), channel_id=1, source_target_pairs={{0,1},{1,0},{2,3},{3,2},{4,5},{5,4},{6,7},{7,6},{8,9},{9,8},{10,11... | collective-permute-start | bytes 1351688 | tf_op jit(solution)/shard_map/ppermute | solution.py:520
  97.2 38.3 %collective-permute-start.16 = (bf16[176,1280]{1,0:T(8,128)(2,1)}, bf16[176,1280]{1,0:T(8,128)(2,1)}, u32[]{:S(2)}, u32[]{:S(2)}) collective-permute-start(bf16[176,1280]{1,0:T(8,128)(2,1)} %slice.107), channel_id=1, source_target_pairs={{0,2},{1,3},{2,0},{3,1},{4,6},{5,7},{6,4},{7,5},{8,10},{9,11},{10,... | collective-permute-start | bytes 1351688 | tf_op jit(solution)/shard_map/ppermute | solution.py:520
  99.5 38.4 %collective-permute-start.17 = (bf16[176,1280]{1,0:T(8,128)(2,1)}, bf16[176,1280]{1,0:T(8,128)(2,1)}, u32[]{:S(2)}, u32[]{:S(2)}) collective-permute-start(bf16[176,1280]{1,0:T(8,128)(2,1)} %slice.107), channel_id=1, source_target_pairs={{0,3},{1,2},{2,1},{3,0},{4,7},{5,6},{6,5},{7,4},{8,11},{9,10},{10,... | collective-permute-start | bytes 1351688 | tf_op jit(solution)/shard_map/ppermute | solution.py:520
  99.7 38.2 %collective-permute-start.13 = (bf16[2,640,640]{2,1,0:T(8,128)(2,1)}, bf16[2,640,640]{2,1,0:T(8,128)(2,1)S(1)}, u32[]{:S(2)}, u32[]{:S(2)}) collective-permute-start(bf16[2,640,640]{2,1,0:T(8,128)(2,1)} %collective-permute-done.refs_3_.refs_10_), channel_id=1, source_target_pairs={{0,8},{4,12},{8,0},{12,4},{16,24},{20,28},{24,16},{28,20},{1,9},{5... | collective-permute-start | bytes 4915208 | tf_op jit(solution)/shard_map/ppermute | solution.py:517
  99.9 38.0 %collective-permute-start.14 = (bf16[624,1280]{1,0:T(8,128)(2,1)}, bf16[624,1280]{1,0:T(8,128)(2,1)S(1)}, u32[]{:S(2)}, u32[]{:S(2)}) collective-permute-start(bf16[624,1280]{1,0:T(8,128)(2,1)} %bitcast.3), channel_id=1, source_target_pairs={{0,16},{4,20},{8,24},{12,28},{16,0},{20,4},{24,8},{28,12},{1,17},{... | collective-permute-start | bytes 4792328 | tf_op jit(solution)/shard_map/ppermute | solution.py:517
  137.9 15.5 %copy-start.3 = (bf16[624,1280]{1,0:T(8,128)(2,1)}, bf16[624,1280]{1,0:T(8,128)(2,1)S(1)}, u32[]{:S(2)}) copy-start(bf16[624,1280]{1,0:T(8,128)(2,1)S(1)} %collective-permute-done.14.refs_5_.refs_6_.refs_7_) | copy-start | bytes 4792324
  137.9 7.0 %copy-start.6 = (bf16[2,640,640]{2,1,0:T(8,128)(2,1)}, bf16[2,640,640]{2,1,0:T(8,128)(2,1)S(1)}, u32[]{:S(2)}) copy-start(bf16[2,640,640]{2,1,0:T(8,128)(2,1)S(1)} %collective-permute-done.13.refs_1_.refs_16_) | copy-start | bytes 4915204
  137.9 7.0 %collective-permute-start.18 = (bf16[2,640,640]{2,1,0:T(8,128)(2,1)S(1)}, bf16[2,640,640]{2,1,0:T(8,128)(2,1)}, u32[]{:S(2)}, u32[]{:S(2)}) collective-permute-start(bf16[2,640,640]{2,1,0:T(8,128)(2,1)S(1)} %collective-permute-done.13.refs_1_.refs_16_), channel_id=1, source_target_pairs={{0,4},{4,0},{8,12},{12,8},{16,20},{20,16},{24,28},{28,24},{1,5},{5... | collective-permute-start | bytes 4915208 | tf_op jit(solution)/shard_map/ppermute | solution.py:517
  140.4 4.5 %collective-permute-start.19 = (bf16[1,640,640]{2,1,0:T(8,128)(2,1)}, bf16[1,640,640]{2,1,0:T(8,128)(2,1)}, u32[]{:S(2)}, u32[]{:S(2)}) collective-permute-start(bf16[1,640,640]{2,1,0:T(8,128)(2,1)} %collective-permute-done.8.refs_2_.refs_17_), channel_id=1, source_target_pairs={{0,4},{4,0},{8,12},{12,8},{16,20},{20,16},{24,28},{28,24},{1,5},{5... | collective-permute-start | bytes 2457608 | tf_op jit(solution)/shard_map/ppermute | solution.py:517
  153.4 17.0 %copy-start.16 = (f32[2,384]{1,0:T(2,128)S(1)}, f32[2,384]{1,0:T(2,128)}, u32[]{:S(2)}) copy-start(f32[2,384]{1,0:T(2,128)} %get-tuple-element.112) | copy-start | bytes 9220
  153.4 25.0 %copy-start = (bf16[2,384,640]{2,1,0:T(8,128)(2,1)S(1)}, bf16[2,384,640]{2,1,0:T(8,128)(2,1)}, u32[]{:S(2)}) copy-start(bf16[2,384,640]{2,1,0:T(8,128)(2,1)} %get-tuple-element.126.refs_0_.refs_8_) | copy-start | bytes 2949124
  153.5 34.0 %collective-permute-start.23 = (bf16[2,384,640]{2,1,0:T(8,128)(2,1)}, bf16[2,384,640]{2,1,0:T(8,128)(2,1)S(1)}, u32[]{:S(2)}, u32[]{:S(2)}) collective-permute-start(bf16[2,384,640]{2,1,0:T(8,128)(2,1)} %get-tuple-element.126.refs_0_.refs_8_), channel_id=1, source_target_pairs={{0,8},{4,12},{8,0},{12,4},{16,24},{20,28},{24,16},{28,20},{1,9},{5... | collective-permute-start | bytes 2949128 | tf_op jit(solution)/shard_map/ppermute | solution.py:517
  169.6 19.2 %copy-start.7 = (bf16[1,384,640]{2,1,0:T(8,128)(2,1)S(1)}, bf16[1,384,640]{2,1,0:T(8,128)(2,1)}, u32[]{:S(2)}) copy-start(bf16[1,384,640]{2,1,0:T(8,128)(2,1)} %get-tuple-element.127.refs_4_.refs_12_) | copy-start | bytes 1474564
  170.4 2.8 %collective-permute-start.20 = (f32[2,2,384]{2,0,1:T(2,128)S(1)}, f32[2,2,384]{2,0,1:T(2,128)S(1)}, u32[]{:S(2)}, u32[]{:S(2)}) collective-permute-start(f32[2,2,384]{2,0,1:T(2,128)S(1)} %pad_maximum_fusion.3), channel_id=1, source_target_pairs={{0,16},{4,20},{8,24},{12,28},{16,0},{20,4},{24,8},{28,12},{1,17},{... | collective-permute-start | bytes 18440 | tf_op jit(solution)/shard_map/ppermute | solution.py:517
  171.7 15.7 %collective-permute-start.24 = (bf16[1,384,640]{2,1,0:T(8,128)(2,1)}, bf16[1,384,640]{2,1,0:T(8,128)(2,1)}, u32[]{:S(2)}, u32[]{:S(2)}) collective-permute-start(bf16[1,384,640]{2,1,0:T(8,128)(2,1)} %get-tuple-element.127.refs_4_.refs_12_), channel_id=1, source_target_pairs={{0,8},{4,12},{8,0},{12,4},{16,24},{20,28},{24,16},{28,20},{1,9},{5... | collective-permute-start | bytes 1474568 | tf_op jit(solution)/shard_map/ppermute | solution.py:517
  173.4 2.8 %collective-permute-start.21 = (f32[2,2,384]{2,0,1:T(2,128)S(1)}, f32[2,2,384]{2,0,1:T(2,128)S(1)}, u32[]{:S(2)}, u32[]{:S(2)}) collective-permute-start(f32[2,2,384]{2,0,1:T(2,128)S(1)} %fusion.14), channel_id=1, source_target_pairs={{0,1},{1,0},{2,3},{3,2},{4,5},{5,4},{6,7},{7,6},{8,9},{9,8},{10,11... | collective-permute-start | bytes 18440 | tf_op jit(solution)/shard_map/ppermute | solution.py:520
  176.2 4.8 %collective-permute-start.22 = (f32[2,2,384]{2,0,1:T(2,128)S(1)}, f32[2,2,384]{2,0,1:T(2,128)S(1)}, u32[]{:S(2)}, u32[]{:S(2)}) collective-permute-start(f32[2,2,384]{2,0,1:T(2,128)S(1)} %fusion.24), channel_id=1, source_target_pairs={{0,2},{1,3},{2,0},{3,1},{4,6},{5,7},{6,4},{7,5},{8,10},{9,11},{10,... | collective-permute-start | bytes 18440 | tf_op jit(solution)/shard_map/ppermute | solution.py:520
  178.4 15.7 %collective-permute-start.25 = (bf16[2,384,640]{2,1,0:T(8,128)(2,1)S(1)}, bf16[2,384,640]{2,1,0:T(8,128)(2,1)S(1)}, u32[]{:S(2)}, u32[]{:S(2)}) collective-permute-start(bf16[2,384,640]{2,1,0:T(8,128)(2,1)S(1)} %copy-done), channel_id=1, source_target_pairs={{0,4},{4,0},{8,12},{12,8},{16,20},{20,16},{24,28},{28,24},{1,5},{5... | collective-permute-start | bytes 2949128 | tf_op jit(solution)/shard_map/ppermute | solution.py:517
  187.4 8.4 %copy-start.1 = (bf16[2,384,640]{2,1,0:T(8,128)(2,1)}, bf16[2,384,640]{2,1,0:T(8,128)(2,1)S(1)}, u32[]{:S(2)}) copy-start(bf16[2,384,640]{2,1,0:T(8,128)(2,1)S(1)} %collective-permute-done.23.refs_2_.refs_10_) | copy-start | bytes 2949124
  187.4 8.4 %collective-permute-start.26 = (bf16[2,384,640]{2,1,0:T(8,128)(2,1)S(1)}, bf16[2,384,640]{2,1,0:T(8,128)(2,1)}, u32[]{:S(2)}, u32[]{:S(2)}) collective-permute-start(bf16[2,384,640]{2,1,0:T(8,128)(2,1)S(1)} %collective-permute-done.23.refs_2_.refs_10_), channel_id=1, source_target_pairs={{0,4},{4,0},{8,12},{12,8},{16,20},{20,16},{24,28},{28,24},{1,5},{5... | collective-permute-start | bytes 2949128 | tf_op jit(solution)/shard_map/ppermute | solution.py:517
  188.5 2.4 collective-permute-start.33
  188.9 5.2 %collective-permute-start.29 = (bf16[1,384,640]{2,1,0:T(8,128)(2,1)S(1)}, bf16[1,384,640]{2,1,0:T(8,128)(2,1)}, u32[]{:S(2)}, u32[]{:S(2)}) collective-permute-start(bf16[1,384,640]{2,1,0:T(8,128)(2,1)S(1)} %copy-done.7), channel_id=1, source_target_pairs={{0,4},{4,0},{8,12},{12,8},{16,20},{20,16},{24,28},{28,24},{1,5},{5... | collective-permute-start | bytes 1474568 | tf_op jit(solution)/shard_map/ppermute | solution.py:517
  191.0 2.0 collective-permute-start.34
  192.2 1.2 collective-permute-start.32
  193.0 12.8 %collective-permute-start.28 = (bf16[1,384,640]{2,1,0:T(8,128)(2,1)}, bf16[1,384,640]{2,1,0:T(8,128)(2,1)}, u32[]{:S(2)}, u32[]{:S(2)}) collective-permute-start(bf16[1,384,640]{2,1,0:T(8,128)(2,1)} %get-tuple-element.132.refs_4_), channel_id=1, source_target_pairs={{0,8},{4,12},{8,0},{12,4},{16,24},{20,28},{24,16},{28,20},{1,9},{5... | collective-permute-start | bytes 1474568 | tf_op jit(solution)/shard_map/ppermute | solution.py:517
  193.4 2.4 collective-permute-start.30
  194.0 15.5 %collective-permute-start.27 = (bf16[1,384,640]{2,1,0:T(8,128)(2,1)}, bf16[1,384,640]{2,1,0:T(8,128)(2,1)S(1)}, u32[]{:S(2)}, u32[]{:S(2)}) collective-permute-start(bf16[1,384,640]{2,1,0:T(8,128)(2,1)} %get-tuple-element.132.refs_4_), channel_id=1, source_target_pairs={{0,4},{4,0},{8,12},{12,8},{16,20},{20,16},{24,28},{28,24},{1,5},{5... | collective-permute-start | bytes 1474568 | tf_op jit(solution)/shard_map/ppermute | solution.py:517
  194.1 1.7 copy-start.2
  205.8 3.7 %collective-permute-start.31 = (bf16[1,384,640]{2,1,0:T(8,128)(2,1)}, bf16[1,384,640]{2,1,0:T(8,128)(2,1)S(1)}, u32[]{:S(2)}, u32[]{:S(2)}) collective-permute-start(bf16[1,384,640]{2,1,0:T(8,128)(2,1)} %collective-permute-done.28.refs_6_), channel_id=1, source_target_pairs={{0,4},{4,0},{8,12},{12,8},{16,20},{20,16},{24,28},{28,24},{1,5},{5... | collective-permute-start | bytes 1474568 | tf_op jit(solution)/shard_map/ppermute | solution.py:517
  207.7 33.9 %collective-permute-start.37 = (bf16[3,128,640]{2,1,0:T(8,128)(2,1)}, bf16[3,128,640]{2,1,0:T(8,128)(2,1)S(1)}, u32[]{:S(2)}, u32[]{:S(2)}) collective-permute-start(bf16[3,128,640]{2,1,0:T(8,128)(2,1)} %get-tuple-element.151), channel_id=1, source_target_pairs={{0,16},{4,20},{8,24},{12,28},{16,0},{20,4},{24,8},{28,12},{1,17},{... | collective-permute-start | bytes 1474568 | tf_op jit(solution)/shard_map/ppermute | solution.py:517
  209.5 0.8 copy-start.8
  210.3 0.8 copy-start.9
  214.3 27.5 %collective-permute-start.36 = (bf16[3,128,640]{2,1,0:T(8,128)(2,1)}, bf16[3,128,640]{2,1,0:T(8,128)(2,1)S(1)}, u32[]{:S(2)}, u32[]{:S(2)}) collective-permute-start(bf16[3,128,640]{2,1,0:T(8,128)(2,1)} %get-tuple-element.149), channel_id=1, source_target_pairs={{0,16},{4,20},{8,24},{12,28},{16,0},{20,4},{24,8},{28,12},{1,17},{... | collective-permute-start | bytes 1474568 | tf_op jit(solution)/shard_map/ppermute | solution.py:517
  227.4 14.3 %copy-start.12 = (bf16[3,128,640]{2,1,0:T(8,128)(2,1)S(1)}, bf16[3,128,640]{2,1,0:T(8,128)(2,1)}, u32[]{:S(2)}) copy-start(bf16[3,128,640]{2,1,0:T(8,128)(2,1)} %get-tuple-element.150) | copy-start | bytes 1474564
  227.4 17.0 %collective-permute-start.35 = (bf16[384,640]{1,0:T(8,128)(2,1)}, bf16[384,640]{1,0:T(8,128)(2,1)S(1)}, u32[]{:S(2)}, u32[]{:S(2)}) collective-permute-start(bf16[384,640]{1,0:T(8,128)(2,1)} %attend.2), channel_id=1, source_target_pairs={{0,16},{4,20},{8,24},{12,28},{16,0},{20,4},{24,8},{28,12},{1,17},{... | collective-permute-start | bytes 1474568 | tf_op jit(solution)/shard_map/ppermute | solution.py:517
  241.6 1.0 copy-start.13
  242.9 1.5 copy-start.11
Sparse Core Ops, SparseCore 0:
  9.6 75.2 all-gather.2

commit v2 on v1

--- a/solution.py
+++ b/solution.py
@@ -693,8 +693,8 @@
     other_values = spread({0: other_value, first: value_ahead}, rest_hops)
     values = [(held[n], 1) for n in range(top)] + [(other_values[n], 0) for n in range(top)]
     values_picked = pick_pages(values, me, pages, None)
-    key_ahead, values_picked = lax.optimization_barrier((key_ahead, values_picked))
     values_other = swap(values_picked[0], top)
+    key_ahead, values_other = lax.optimization_barrier((key_ahead, values_other))
     other_keys = spread({0: other_key, first: key_ahead}, rest_hops)
     keys = [(held[n], 0) for n in range(top)] + [(other_keys[n], 0) for n in range(top)]
     keys_picked = pick_pages(keys, me, pages, scale)

time: 253 us -> 253 us (level)
  Pallas kernels: 79.2 us -> 73.5 us
  waiting for transfers between devices: 85.5 us -> 90.3 us
    pallas_call x2, Pallas kernels: 25.3 us -> 19.7 us  [attend(): pl.pallas_call(functools.partial(attend_kernel, places), in_specs=[smem,...]
    ppermute x30, waiting for transfers between devices: 65.7 us -> 69.9 us  [swap(): return lax.ppermute(value, 'row', [(i, i ^ bit) for i in range(ring)])]
  transfers between devices with their start and end apart: 39 -> 39, of which waited for: 16 -> 18; matrix products, arithmetic and copies ran while one was open for 9% -> 9% of each run, Pallas kernels for 28% -> 25%
where the time goes in v2:
time: 253 us; the launch traced here: 250 us
  waiting for transfers between devices  90.3 us (36%)
  Pallas kernels  73.5 us (29%)
  starting transfers between devices  37.3 us (15%)
  between operations  20.7 us (8%)
  local copies, waits for them, and re-layouts  14.6 us (6%)
  other arithmetic  13.5 us (5%)
    ppermute x30, waiting for transfers between devices, swap(): return lax.ppermute(value, 'row', [(i, i ^ bit) for i in range(ring)])  69.9 us
    pallas_call x3, Pallas kernels, project(): pl.pallas_call(functools.partial(project_kernel, parts, blocks, spots, pa...  39.1 us
    ppermute x30, starting transfers between devices, swap(): return lax.ppermute(value, 'row', [(i, i ^ bit) for i in range(ring)])  26.1 us
    pallas_call x2, Pallas kernels, attend(): pl.pallas_call(functools.partial(attend_kernel, places), in_specs=[smem,...  19.7 us
    ppermute x8, starting transfers between devices, across(): return lax.ppermute(value, 'col', [(c, c ^ step) for c in range(ranks)])  11.1 us
    ppermute x8, waiting for transfers between devices, across(): return lax.ppermute(value, 'col', [(c, c ^ step) for c in range(ranks)])  10 us
    all_gather x1, waiting for transfers between devices, split_heads(): hidden_all = lax.all_gather(hidden, 'col', axis=0)  9.59 us
    pallas_call x2, Pallas kernels, pick_pages(): pl.pallas_call(functools.partial(pages_kernel, tuple((at for _, at in pie...  6.18 us
  transfers between devices with their start and end apart: 39, of which 18 were waited for; matrix products, arithmetic and copies ran while one was open for 9% of the time, Pallas kernels for 25%

profile of v2, /device:TPU:9, one launch (start us, length us, event | category | flops | bytes accessed | tf_op | source)
XLA Modules:
  0.0 249.9 jit_solution(11463816356461598077)
XLA Ops:
  7.2 0.7 all-gather.3.cloned.1.call-update
  7.9 4.8 %cut.1 = (bf16[3,640,640]{2,1,0:T(8,128)(2,1)}, bf16[2,640,640]{2,1,0:T(8,128)(2,1)}, bf16[1,640,640]{2,1,0:T(8,128)(2,1)}) custom-call(s32[1]{0:T(128)} %bitcast.1.half_ref, bf16[640,1280]{1,0:T(8,128)(2,1)} %refs_0_.1, bf16[640,1280]{1,0:T(8,128)(2,1)} %refs_1_.1, bf16[640,1280]{1,0:T(8,128)(2,1)} %refs_2_.1), custom_call_target="tpu_custom_call" | custom-call | bytes 9830400 | tf_op jit(solution)/shard_map/cut/pallas_call | solution.py:72
  12.7 1.3 collective-permute-start.2
  14.0 1.0 collective-permute-start.3
  14.9 1.2 collective-permute-start
  17.0 1.4 collective-permute-start.6
  18.4 1.6 collective-permute-done.6
  20.0 3.9 %collective-permute-start.5 = (f32[2,384]{1,0:T(2,128)S(1)}, f32[2,384]{1,0:T(2,128)S(1)}, u32[]{:S(2)}, u32[]{:S(2)}) collective-permute-start(f32[2,384]{1,0:T(2,128)S(1)} %pad_maximum_fusion.4), channel_id=1, source_target_pairs={{0,2},{1,3},{2,0},{3,1},{4,6},{5,7},{6,4},{7,5},{8,10},{9,11},{10,... | collective-permute-start | bytes 9224 | tf_op jit(solution)/shard_map/ppermute | solution.py:520
  23.8 1.4 collective-permute-done.5
  25.3 1.6 collective-permute-start.4
  26.8 1.4 collective-permute-done.4
  28.3 1.3 collective-permute-start.7
  29.6 40.8 %collective-permute-done.7 = f32[5,384]{1,0:T(8,128)S(1)} collective-permute-done((f32[5,384]{1,0:T(8,128)S(1)}, f32[5,384]{1,0:T(8,128)S(1)}, u32[]{:S(2)}, u32[]{:S(2)}) %collective-permute-start.7) | collective-permute-done | bytes 7712 | tf_op jit(solution)/shard_map/ppermute | solution.py:517
  70.4 0.9 copy-done.11
  71.3 0.8 collective-permute-start.12
  72.2 1.2 collective-permute-start.9
  73.7 1.0 collective-permute-start.11
  75.3 9.6 %all-gather.3.cloned.1.call-done = bf16[1536,1280]{1,0:T(8,128)(2,1)} async-done(((bf16[384,1280]{1,0:T(8,128)(2,1)}), bf16[1536,1280]{1,0:T(8,128)(2,1)}) %all-gather.3.cloned.1.call-update) | async-done | bytes 3932176 | tf_op jit(solution)/shard_map/all_gather | solution.py:534
  84.9 1.5 constant_dynamic-slice_fusion.10
  86.4 1.3 pad_maximum_fusion.1
  87.7 5.1 %collective-permute-done.8.refs_2_.refs_17_ = bf16[1,640,640]{2,1,0:T(8,128)(2,1)} collective-permute-done((bf16[1,640,640]{2,1,0:T(8,128)(2,1)}, bf16[1,640,640]{2,1,0:T(8,128)(2,1)}, u32[]{:S(2)}, u32[]{:S(2)}) %collective-permute-start.8) | collective-permute-done | bytes 819232 | tf_op jit(solution)/shard_map/ppermute | solution.py:517
  92.8 2.4 collective-permute-done.9.refs_0_.refs_4_
  95.2 1.8 slice.107
  97.2 2.3 collective-permute-start.16
  99.9 1.2 collective-permute-start.14
  101.2 0.6 fusion.22
  101.9 0.6 fusion.21
  102.5 3.8 %convert_reduce_fusion.2 = (s32[]{:T(128)}, s32[]{:T(128)}, s32[]{:T(128)}, s32[]{:T(128)}, f32[3072]{0:T(1024)}) fusion(s32[3072]{0:T(1024)S(1)} %copy-done.15, s32[]{:T(128)} %bitcast.9, s32[]{:T(128)} %bitcast.11, s32[]{:T(128)} %bitcast.7, s32[]{:T(128)} %bitcast.5), kind=kLoop, calls=%fused_computation.23 | loop fusion | flops 39932 | bytes 24608 | tf_op jit(solution)/shard_map/reduce_sum | solution.py:353
  115.5 0.6 scatter_custom_fusion
  116.9 0.6 pad_add_fusion.1
  117.6 2.7 %fusion.4 = (f32[384,128]{1,0:T(8,128)}, f32[384,128]{1,0:T(8,128)}, f32[384,128]{1,0:T(8,128)}, f32[384,128]{1,0:T(8,128)}, f32[384,128]{1,0:T(8,128)}, /*index=5*/f32[384,128]{1,0:T(8,128)}) fusion(f32[384]{0:T(512)S(1)} %get-tuple-element.155, f32[384]{0:T(512)S(1)} %get-tuple-element.156, f32[384]{0:T(512)S(1)} %get-tuple-element.154, ...), kind=kLoop, calls=%fused_computation.14 | loop fusion | flops 786432 | bytes 1190784 | tf_op jit(solution)/shard_map/jit(_where)/select_n | solution.py:38
  120.3 14.7 %project.3.refs_5_ = f32[384,1920]{1,0:T(8,128)} custom-call(s32[2]{0:T(128)} %pad_add_fusion.3.place_ref, f32[2,384]{1,0:T(2,128)} %slice.118.stats_ref, f32[2,5120]{1,0:T(2,128)} %modulation_ref.5, bf16[4,384,1280]{2,1,0:T(8,128)(2,1)} %bitcast.23, bf16[3,640,640]{2,1,0:T(8,128)(2,1)} %get-tuple-element.96.refs_1_.refs_8_, bf16[3,640,640]{2,1,0:T(8,128)(2,1)} %copy-done.4, ...), custom_call_target="tpu_custom_call" | custom-call | flops 5662310400 | bytes 20643840 | tf_op jit(solution)/shard_map/project/pallas_call | solution.py:223
  135.0 2.9 %collective-permute-done.17.refs_3_ = bf16[176,1280]{1,0:T(8,128)(2,1)} collective-permute-done((bf16[176,1280]{1,0:T(8,128)(2,1)}, bf16[176,1280]{1,0:T(8,128)(2,1)}, u32[]{:S(2)}, u32[]{:S(2)}) %collective-permute-start.17) | collective-permute-done | bytes 450592 | tf_op jit(solution)/shard_map/ppermute | solution.py:520
  137.9 2.5 collective-permute-start.18
  141.1 3.8 %collective-permute-done.19.refs_4_.refs_19_ = bf16[1,640,640]{2,1,0:T(8,128)(2,1)} collective-permute-done((bf16[1,640,640]{2,1,0:T(8,128)(2,1)}, bf16[1,640,640]{2,1,0:T(8,128)(2,1)}, u32[]{:S(2)}, u32[]{:S(2)}) %collective-permute-start.19) | collective-permute-done | bytes 819232 | tf_op jit(solution)/shard_map/ppermute | solution.py:517
  144.9 8.5 %project.4 = (f32[384,640]{1,0:T(8,128)}, f32[2,384]{1,0:T(2,128)}, bf16[2,384,640]{2,1,0:T(8,128)(2,1)}) custom-call(s32[2]{0:T(128)} %pad_add_fusion.3.place_ref, f32[2,384]{1,0:T(2,128)} %slice.118.stats_ref, f32[2,5120]{1,0:T(2,128)} %modulation_ref.5, bf16[4,384,1280]{2,1,0:T(8,128)(2,1)} %bitcast.24, bf16[2,640,640]{2,1,0:T(8,128)(2,1)} %copy-done.6, ...), custom_call_target="tpu_custom_call" | custom-call | flops 1887436800 | bytes 8847360 | tf_op jit(solution)/shard_map/project/pallas_call | solution.py:223
  153.8 15.9 %project.5 = (f32[384,640]{1,0:T(8,128)}, f32[2,384]{1,0:T(2,128)}, bf16[1,384,640]{2,1,0:T(8,128)(2,1)}, bf16[1,384,640]{2,1,0:T(8,128)(2,1)}) custom-call(s32[2]{0:T(128)} %pad_add_fusion.3.place_ref, f32[2,384]{1,0:T(2,128)} %slice.119.stats_ref, f32[2,5120]{1,0:T(2,128)} %modulation_ref.5, bf16[384,1280]{1,0:T(8,128)(2,1)} %collective-permute-done.9.refs_0_.refs_4_, ...), custom_call_target="tpu_custom_call" | custom-call | flops 7549747200 | bytes 26542080 | tf_op jit(solution)/shard_map/project/pallas_call | solution.py:223
  169.7 0.7 stack.62
  170.4 1.3 collective-permute-start.20
  171.7 1.3 collective-permute-start.24
  173.4 2.8 %collective-permute-done.21 = f32[2,2,384]{2,0,1:T(2,128)S(1)} collective-permute-done((f32[2,2,384]{2,0,1:T(2,128)S(1)}, f32[2,2,384]{2,0,1:T(2,128)S(1)}, u32[]{:S(2)}, u32[]{:S(2)}) %collective-permute-start.21) | collective-permute-done | bytes 6176 | tf_op jit(solution)/shard_map/ppermute | solution.py:520
  176.2 1.6 collective-permute-start.22
  177.8 2.6 %collective-permute-start.25 = (bf16[2,384,640]{2,1,0:T(8,128)(2,1)S(1)}, bf16[2,384,640]{2,1,0:T(8,128)(2,1)S(1)}, u32[]{:S(2)}, u32[]{:S(2)}) collective-permute-start(bf16[2,384,640]{2,1,0:T(8,128)(2,1)S(1)} %copy-done), channel_id=1, source_target_pairs={{0,4},{4,0},{8,12},{12,8},{16,20},{20,16},{24,28},{28,24},{1,5},{5... | collective-permute-start | bytes 2949128 | tf_op jit(solution)/shard_map/ppermute | solution.py:517
  181.0 3.9 %turn.1 = (bf16[384,640]{1,0:T(8,128)(2,1)}, bf16[384,640]{1,0:T(8,128)(2,1)}) custom-call(f32[2,384]{1,0:T(2,128)} %get-tuple-element.186.squares_ref, f32[1,640]{1,0:T(1,128)} %broadcast_in_dim.76.gain_ref, f32[384,640]{1,0:T(8,128)} %get-tuple-element.121.refs_0_, f32[384,640]{1,0:T(8,128)} %get-tuple-element.122.refs_1_, ...), custom_call_target="tpu_custom_call" | custom-call | tf_op jit(solution)/shard_map/turn/pallas_call | solution.py:274
  184.9 2.6 %collective-permute-done.24.refs_6_.refs_14_ = bf16[1,384,640]{2,1,0:T(8,128)(2,1)} collective-permute-done((bf16[1,384,640]{2,1,0:T(8,128)(2,1)}, bf16[1,384,640]{2,1,0:T(8,128)(2,1)}, u32[]{:S(2)}, u32[]{:S(2)}) %collective-permute-start.24) | collective-permute-done | bytes 491552 | tf_op jit(solution)/shard_map/ppermute | solution.py:517
  187.4 1.1 collective-permute-start.26
  189.4 2.1 collective-permute-done.34
  191.5 1.2 collective-permute-start.35
  193.7 3.0 %pick_pages.2 = (bf16[3,128,640]{2,1,0:T(8,128)(2,1)}, bf16[3,128,640]{2,1,0:T(8,128)(2,1)}) custom-call(s32[1]{0:T(128)} %bitcast.me_ref, s32[6]{0:T(128)} %pad_add_fusion.page_ref, bf16[2,384,640]{2,1,0:T(8,128)(2,1)} %get-tuple-element.125.refs_0_.refs_8_, bf16[2,384,640]{2,1,0:T(8,128)(2,1)} %copy-done.2, bf16[2,384,640]{2,1,0:T(8,128)(2,1)} %copy-done.1, ...), custom_call_target="tpu_custom_call" | custom-call | tf_op jit(solution)/shard_map/pick_pages/pallas_call | solution.py:433
  196.7 1.3 collective-permute-start.31
  198.0 0.7 collective-permute-start.33
  198.8 0.8 collective-permute-done.33
  199.6 5.8 %collective-permute-done.28.refs_6_ = bf16[1,384,640]{2,1,0:T(8,128)(2,1)S(1)} collective-permute-done((bf16[1,384,640]{2,1,0:T(8,128)(2,1)}, bf16[1,384,640]{2,1,0:T(8,128)(2,1)S(1)}, u32[]{:S(2)}, u32[]{:S(2)}) %collective-permute-start.28) | collective-permute-done | bytes 491552 | tf_op jit(solution)/shard_map/ppermute | solution.py:517
  205.4 4.0 %collective-permute-done.31 = bf16[3,128,640]{2,1,0:T(8,128)(2,1)S(1)} collective-permute-done((bf16[3,128,640]{2,1,0:T(8,128)(2,1)}, bf16[3,128,640]{2,1,0:T(8,128)(2,1)S(1)}, u32[]{:S(2)}, u32[]{:S(2)}) %collective-permute-start.31) | collective-permute-done | bytes 491552 | tf_op jit(solution)/shard_map/ppermute | solution.py:517
  209.4 1.3 collective-permute-start.32
  210.7 0.6 reshape.211.refs_8_
  212.8 0.8 copy-done.10
  213.6 3.2 %pick_pages.3 = (bf16[3,128,640]{2,1,0:T(8,128)(2,1)}, bf16[3,128,640]{2,1,0:T(8,128)(2,1)}) custom-call(s32[1]{0:T(128)} %bitcast.me_ref, s32[6]{0:T(128)} %pad_add_fusion.page_ref, bf16[2,384,640]{2,1,0:T(8,128)(2,1)} %get-tuple-element.125.refs_0_.refs_8_, bf16[2,384,640]{2,1,0:T(8,128)(2,1)} %copy-done.2, bf16[2,384,640]{2,1,0:T(8,128)(2,1)} %copy-done.1, ...), custom_call_target="tpu_custom_call" | custom-call | tf_op jit(solution)/shard_map/pick_pages/pallas_call | solution.py:433
  216.8 1.3 collective-permute-start.37
  218.3 10.8 %attend.2 = bf16[384,640]{1,0:T(8,128)(2,1)} custom-call(s32[1]{0:T(128)} %bitcast.me_ref, s32[2]{0:T(128)} %get-tuple-element.140.bounds_ref, bf16[384,640]{1,0:T(8,128)(2,1)} %get-tuple-element.139.q_ref, bf16[2,384,640]{2,1,0:T(8,128)(2,1)} %get-tuple-element.125.refs_0_.refs_8_, bf16[2,384,640]{2,1,0:T(8,128)(2,1)} %copy-done.2, ...), custom_call_target="tpu_custom_call" | custom-call | flops 1509949440 | bytes 8847360 | tf_op jit(solution)/shard_map/attend/pallas_call | solution.py:368
  229.2 8.9 %attend.3 = bf16[384,640]{1,0:T(8,128)(2,1)} custom-call(s32[1]{0:T(128)} %bitcast.me_ref, s32[2]{0:T(128)} %get-tuple-element.103.bounds_ref, bf16[384,640]{1,0:T(8,128)(2,1)} %get-tuple-element.143.q_ref, bf16[2,384,640]{2,1,0:T(8,128)(2,1)} %get-tuple-element.125.refs_0_.refs_8_, bf16[2,384,640]{2,1,0:T(8,128)(2,1)} %copy-done.2, ...), custom_call_target="tpu_custom_call" | custom-call | flops 1509949440 | bytes 8847360 | tf_op jit(solution)/shard_map/attend/pallas_call | solution.py:368
  238.3 1.4 pad_maximum_fusion
  239.8 2.1 collective-permute-done.36
  241.9 1.2 maximum_select_fusion
  (126 shorter events, 12.3 us)
Async XLA Ops:
  7.2 77.7 %all-gather.3.cloned.1.call-start = ((), (), s32[]{:S(2)}) async-start(), calls=%async_computation | async-start | bytes 4915200 | tf_op jit(solution)/shard_map/all_gather | solution.py:534
  7.9 8.5 %copy-start.5 = (bf16[384,1280]{1,0:T(8,128)(2,1)S(1)}, bf16[384,1280]{1,0:T(8,128)(2,1)}, u32[]{:S(2)}) copy-start(bf16[384,1280]{1,0:T(8,128)(2,1)} %param.10) | copy-start | bytes 2949124
  12.7 14.1 %copy-start.16 = (s32[3,384]{1,0:T(4,128)S(1)}, s32[3,384]{1,0:T(4,128)}, u32[]{:S(2)}) copy-start(s32[3,384]{1,0:T(4,128)} %param.17) | copy-start | bytes 13828
  12.7 57.7 %collective-permute-start.2 = (bf16[3,640,640]{2,1,0:T(8,128)(2,1)}, bf16[3,640,640]{2,1,0:T(8,128)(2,1)S(1)}, u32[]{:S(2)}, u32[]{:S(2)}) collective-permute-start(bf16[3,640,640]{2,1,0:T(8,128)(2,1)} %get-tuple-element.96.refs_1_.refs_8_), channel_id=1, source_target_pairs={{0,8},{4,12},{8,0},{12,4},{16,24},{20,28},{24,16},{28,20},{1,9},{5... | collective-permute-start | bytes 7372808 | tf_op jit(solution)/shard_map/ppermute | solution.py:517
  14.0 57.3 %collective-permute-start.3 = (bf16[3,640,640]{2,1,0:T(8,128)(2,1)}, bf16[3,640,640]{2,1,0:T(8,128)(2,1)}, u32[]{:S(2)}, u32[]{:S(2)}) collective-permute-start(bf16[3,640,640]{2,1,0:T(8,128)(2,1)} %get-tuple-element.96.refs_1_.refs_8_), channel_id=1, source_target_pairs={{0,4},{4,0},{8,12},{12,8},{16,20},{20,16},{24,28},{28,24},{1,5},{5... | collective-permute-start | bytes 7372808 | tf_op jit(solution)/shard_map/ppermute | solution.py:517
  14.9 55.5 %collective-permute-start = (bf16[2,640,640]{2,1,0:T(8,128)(2,1)}, bf16[2,640,640]{2,1,0:T(8,128)(2,1)}, u32[]{:S(2)}, u32[]{:S(2)}) collective-permute-start(bf16[2,640,640]{2,1,0:T(8,128)(2,1)} %get-tuple-element.76), channel_id=1, source_target_pairs={{0,16},{4,20},{8,24},{12,28},{16,0},{20,4},{24,8},{28,12},{1,17},{... | collective-permute-start | bytes 4915208 | tf_op jit(solution)/shard_map/ppermute | solution.py:517
  16.2 54.2 %collective-permute-start.1 = (bf16[1,640,640]{2,1,0:T(8,128)(2,1)}, bf16[1,640,640]{2,1,0:T(8,128)(2,1)S(1)}, u32[]{:S(2)}, u32[]{:S(2)}) collective-permute-start(bf16[1,640,640]{2,1,0:T(8,128)(2,1)} %get-tuple-element.77), channel_id=1, source_target_pairs={{0,16},{4,20},{8,24},{12,28},{16,0},{20,4},{24,8},{28,12},{1,17},{... | collective-permute-start | bytes 2457608 | tf_op jit(solution)/shard_map/ppermute | solution.py:517
  17.0 2.9 %collective-permute-start.6 = (f32[2,384]{1,0:T(2,128)S(1)}, f32[2,384]{1,0:T(2,128)S(1)}, u32[]{:S(2)}, u32[]{:S(2)}) collective-permute-start(f32[2,384]{1,0:T(2,128)S(1)} %pad_maximum_fusion.4), channel_id=1, source_target_pairs={{0,3},{1,2},{2,1},{3,0},{4,7},{5,6},{6,5},{7,4},{8,11},{9,10},{10,... | collective-permute-start | bytes 9224 | tf_op jit(solution)/shard_map/ppermute | solution.py:520
  20.0 5.3 %collective-permute-start.5 = (f32[2,384]{1,0:T(2,128)S(1)}, f32[2,384]{1,0:T(2,128)S(1)}, u32[]{:S(2)}, u32[]{:S(2)}) collective-permute-start(f32[2,384]{1,0:T(2,128)S(1)} %pad_maximum_fusion.4), channel_id=1, source_target_pairs={{0,2},{1,3},{2,0},{3,1},{4,6},{5,7},{6,4},{7,5},{8,10},{9,11},{10,... | collective-permute-start | bytes 9224 | tf_op jit(solution)/shard_map/ppermute | solution.py:520
  25.3 3.0 %collective-permute-start.4 = (f32[2,384]{1,0:T(2,128)S(1)}, f32[2,384]{1,0:T(2,128)S(1)}, u32[]{:S(2)}, u32[]{:S(2)}) collective-permute-start(f32[2,384]{1,0:T(2,128)S(1)} %pad_maximum_fusion.4), channel_id=1, source_target_pairs={{0,1},{1,0},{2,3},{3,2},{4,5},{5,4},{6,7},{7,6},{8,9},{9,8},{10,11... | collective-permute-start | bytes 9224 | tf_op jit(solution)/shard_map/ppermute | solution.py:520
  28.3 42.1 %collective-permute-start.7 = (f32[5,384]{1,0:T(8,128)S(1)}, f32[5,384]{1,0:T(8,128)S(1)}, u32[]{:S(2)}, u32[]{:S(2)}) collective-permute-start(f32[5,384]{1,0:T(8,128)S(1)} %pad_maximum_fusion.2), channel_id=1, source_target_pairs={{0,16},{4,20},{8,24},{12,28},{16,0},{20,4},{24,8},{28,12},{1,17},{... | collective-permute-start | bytes 23048 | tf_op jit(solution)/shard_map/ppermute | solution.py:517
  70.4 0.9 copy-start.11
  71.3 16.4 %copy-start.4 = (bf16[3,640,640]{2,1,0:T(8,128)(2,1)}, bf16[3,640,640]{2,1,0:T(8,128)(2,1)S(1)}, u32[]{:S(2)}) copy-start(bf16[3,640,640]{2,1,0:T(8,128)(2,1)S(1)} %collective-permute-done.2.refs_2_.refs_9_) | copy-start | bytes 7372804
  71.3 23.9 %collective-permute-start.12 = (bf16[3,640,640]{2,1,0:T(8,128)(2,1)S(1)}, bf16[3,640,640]{2,1,0:T(8,128)(2,1)}, u32[]{:S(2)}, u32[]{:S(2)}) collective-permute-start(bf16[3,640,640]{2,1,0:T(8,128)(2,1)S(1)} %collective-permute-done.2.refs_2_.refs_9_), channel_id=1, source_target_pairs={{0,4},{4,0},{8,12},{12,8},{16,20},{20,16},{24,28},{28,24},{1,5},{5... | collective-permute-start | bytes 7372808 | tf_op jit(solution)/shard_map/ppermute | solution.py:517
  72.1 23.1 %collective-permute-start.10 = (bf16[2,640,640]{2,1,0:T(8,128)(2,1)}, bf16[2,640,640]{2,1,0:T(8,128)(2,1)}, u32[]{:S(2)}, u32[]{:S(2)}) collective-permute-start(bf16[2,640,640]{2,1,0:T(8,128)(2,1)} %collective-permute-done.refs_3_.refs_10_), channel_id=1, source_target_pairs={{0,4},{4,0},{8,12},{12,8},{16,20},{20,16},{24,28},{28,24},{1,5},{5... | collective-permute-start | bytes 4915208 | tf_op jit(solution)/shard_map/ppermute | solution.py:517
  72.2 23.0 %collective-permute-start.9 = (bf16[384,1280]{1,0:T(8,128)(2,1)S(1)}, bf16[384,1280]{1,0:T(8,128)(2,1)}, u32[]{:S(2)}, u32[]{:S(2)}) collective-permute-start(bf16[384,1280]{1,0:T(8,128)(2,1)S(1)} %copy-done.5), channel_id=1, source_target_pairs={{0,16},{4,20},{8,24},{12,28},{16,0},{20,4},{24,8},{28,12},{1,17},{... | collective-permute-start | bytes 2949128 | tf_op jit(solution)/shard_map/ppermute | solution.py:517
  73.4 19.4 %collective-permute-start.8 = (bf16[1,640,640]{2,1,0:T(8,128)(2,1)}, bf16[1,640,640]{2,1,0:T(8,128)(2,1)}, u32[]{:S(2)}, u32[]{:S(2)}) collective-permute-start(bf16[1,640,640]{2,1,0:T(8,128)(2,1)} %copy-done.11), channel_id=1, source_target_pairs={{0,8},{4,12},{8,0},{12,4},{16,24},{20,28},{24,16},{28,20},{1,9},{5... | collective-permute-start | bytes 2457608 | tf_op jit(solution)/shard_map/ppermute | solution.py:517
  73.7 19.1 %collective-permute-start.11 = (bf16[1,640,640]{2,1,0:T(8,128)(2,1)}, bf16[1,640,640]{2,1,0:T(8,128)(2,1)}, u32[]{:S(2)}, u32[]{:S(2)}) collective-permute-start(bf16[1,640,640]{2,1,0:T(8,128)(2,1)} %copy-done.11), channel_id=1, source_target_pairs={{0,4},{4,0},{8,12},{12,8},{16,20},{20,16},{24,28},{28,24},{1,5},{5... | collective-permute-start | bytes 2457608 | tf_op jit(solution)/shard_map/ppermute | solution.py:517
  86.3 14.8 %copy-start.15 = (s32[3072]{0:T(1024)S(1)}, s32[3072]{0:T(1024)}, u32[]{:S(2)}) copy-start(s32[3072]{0:T(1024)} %param.18) | copy-start | bytes 36868
  86.4 26.2 %copy-start.18 = (f32[1280]{0:T(1024)S(1)}, f32[1280]{0:T(1024)}, u32[]{:S(2)}) copy-start(f32[1280]{0:T(1024)} %param.15) | copy-start | bytes 15364
  86.4 26.8 %copy-start.19 = (f32[1280]{0:T(1024)S(1)}, f32[1280]{0:T(1024)}, u32[]{:S(2)}) copy-start(f32[1280]{0:T(1024)} %param.16) | copy-start | bytes 15364
  86.4 29.1 %copy-start.20 = (s32[24]{0:T(128)S(1)}, s32[24]{0:T(128)}, u32[]{:S(2)}) copy-start(s32[24]{0:T(128)} %param.19) | copy-start | bytes 292
  97.0 37.9 %collective-permute-start.15 = (bf16[176,1280]{1,0:T(8,128)(2,1)}, bf16[176,1280]{1,0:T(8,128)(2,1)}, u32[]{:S(2)}, u32[]{:S(2)}) collective-permute-start(bf16[176,1280]{1,0:T(8,128)(2,1)} %slice.107), channel_id=1, source_target_pairs={{0,1},{1,0},{2,3},{3,2},{4,5},{5,4},{6,7},{7,6},{8,9},{9,8},{10,11... | collective-permute-start | bytes 1351688 | tf_op jit(solution)/shard_map/ppermute | solution.py:520
  97.2 37.8 %collective-permute-start.16 = (bf16[176,1280]{1,0:T(8,128)(2,1)}, bf16[176,1280]{1,0:T(8,128)(2,1)}, u32[]{:S(2)}, u32[]{:S(2)}) collective-permute-start(bf16[176,1280]{1,0:T(8,128)(2,1)} %slice.107), channel_id=1, source_target_pairs={{0,2},{1,3},{2,0},{3,1},{4,6},{5,7},{6,4},{7,5},{8,10},{9,11},{10,... | collective-permute-start | bytes 1351688 | tf_op jit(solution)/shard_map/ppermute | solution.py:520
  99.5 38.4 %collective-permute-start.17 = (bf16[176,1280]{1,0:T(8,128)(2,1)}, bf16[176,1280]{1,0:T(8,128)(2,1)}, u32[]{:S(2)}, u32[]{:S(2)}) collective-permute-start(bf16[176,1280]{1,0:T(8,128)(2,1)} %slice.107), channel_id=1, source_target_pairs={{0,3},{1,2},{2,1},{3,0},{4,7},{5,6},{6,5},{7,4},{8,11},{9,10},{10,... | collective-permute-start | bytes 1351688 | tf_op jit(solution)/shard_map/ppermute | solution.py:520
  99.7 38.2 %collective-permute-start.13 = (bf16[2,640,640]{2,1,0:T(8,128)(2,1)}, bf16[2,640,640]{2,1,0:T(8,128)(2,1)S(1)}, u32[]{:S(2)}, u32[]{:S(2)}) collective-permute-start(bf16[2,640,640]{2,1,0:T(8,128)(2,1)} %collective-permute-done.refs_3_.refs_10_), channel_id=1, source_target_pairs={{0,8},{4,12},{8,0},{12,4},{16,24},{20,28},{24,16},{28,20},{1,9},{5... | collective-permute-start | bytes 4915208 | tf_op jit(solution)/shard_map/ppermute | solution.py:517
  99.9 38.0 %collective-permute-start.14 = (bf16[624,1280]{1,0:T(8,128)(2,1)}, bf16[624,1280]{1,0:T(8,128)(2,1)S(1)}, u32[]{:S(2)}, u32[]{:S(2)}) collective-permute-start(bf16[624,1280]{1,0:T(8,128)(2,1)} %bitcast.3), channel_id=1, source_target_pairs={{0,16},{4,20},{8,24},{12,28},{16,0},{20,4},{24,8},{28,12},{1,17},{... | collective-permute-start | bytes 4792328 | tf_op jit(solution)/shard_map/ppermute | solution.py:517
  137.9 15.5 %copy-start.3 = (bf16[624,1280]{1,0:T(8,128)(2,1)}, bf16[624,1280]{1,0:T(8,128)(2,1)S(1)}, u32[]{:S(2)}) copy-start(bf16[624,1280]{1,0:T(8,128)(2,1)S(1)} %collective-permute-done.14.refs_5_.refs_6_.refs_7_) | copy-start | bytes 4792324
  137.9 7.0 %copy-start.6 = (bf16[2,640,640]{2,1,0:T(8,128)(2,1)}, bf16[2,640,640]{2,1,0:T(8,128)(2,1)S(1)}, u32[]{:S(2)}) copy-start(bf16[2,640,640]{2,1,0:T(8,128)(2,1)S(1)} %collective-permute-done.13.refs_1_.refs_16_) | copy-start | bytes 4915204
  137.9 7.0 %collective-permute-start.18 = (bf16[2,640,640]{2,1,0:T(8,128)(2,1)S(1)}, bf16[2,640,640]{2,1,0:T(8,128)(2,1)}, u32[]{:S(2)}, u32[]{:S(2)}) collective-permute-start(bf16[2,640,640]{2,1,0:T(8,128)(2,1)S(1)} %collective-permute-done.13.refs_1_.refs_16_), channel_id=1, source_target_pairs={{0,4},{4,0},{8,12},{12,8},{16,20},{20,16},{24,28},{28,24},{1,5},{5... | collective-permute-start | bytes 4915208 | tf_op jit(solution)/shard_map/ppermute | solution.py:517
  140.4 4.5 %collective-permute-start.19 = (bf16[1,640,640]{2,1,0:T(8,128)(2,1)}, bf16[1,640,640]{2,1,0:T(8,128)(2,1)}, u32[]{:S(2)}, u32[]{:S(2)}) collective-permute-start(bf16[1,640,640]{2,1,0:T(8,128)(2,1)} %collective-permute-done.8.refs_2_.refs_17_), channel_id=1, source_target_pairs={{0,4},{4,0},{8,12},{12,8},{16,20},{20,16},{24,28},{28,24},{1,5},{5... | collective-permute-start | bytes 2457608 | tf_op jit(solution)/shard_map/ppermute | solution.py:517
  153.4 17.0 %copy-start.17 = (f32[2,384]{1,0:T(2,128)S(1)}, f32[2,384]{1,0:T(2,128)}, u32[]{:S(2)}) copy-start(f32[2,384]{1,0:T(2,128)} %get-tuple-element.111) | copy-start | bytes 9220
  153.4 24.4 %copy-start = (bf16[2,384,640]{2,1,0:T(8,128)(2,1)S(1)}, bf16[2,384,640]{2,1,0:T(8,128)(2,1)}, u32[]{:S(2)}) copy-start(bf16[2,384,640]{2,1,0:T(8,128)(2,1)} %get-tuple-element.125.refs_0_.refs_8_) | copy-start | bytes 2949124
  153.4 34.0 %collective-permute-start.23 = (bf16[2,384,640]{2,1,0:T(8,128)(2,1)}, bf16[2,384,640]{2,1,0:T(8,128)(2,1)S(1)}, u32[]{:S(2)}, u32[]{:S(2)}) collective-permute-start(bf16[2,384,640]{2,1,0:T(8,128)(2,1)} %get-tuple-element.125.refs_0_.refs_8_), channel_id=1, source_target_pairs={{0,8},{4,12},{8,0},{12,4},{16,24},{20,28},{24,16},{28,20},{1,9},{5... | collective-permute-start | bytes 2949128 | tf_op jit(solution)/shard_map/ppermute | solution.py:517
  169.6 18.9 %copy-start.7 = (bf16[1,384,640]{2,1,0:T(8,128)(2,1)S(1)}, bf16[1,384,640]{2,1,0:T(8,128)(2,1)}, u32[]{:S(2)}) copy-start(bf16[1,384,640]{2,1,0:T(8,128)(2,1)} %get-tuple-element.126.refs_4_.refs_12_) | copy-start | bytes 1474564
  170.4 2.8 %collective-permute-start.20 = (f32[2,2,384]{2,0,1:T(2,128)S(1)}, f32[2,2,384]{2,0,1:T(2,128)S(1)}, u32[]{:S(2)}, u32[]{:S(2)}) collective-permute-start(f32[2,2,384]{2,0,1:T(2,128)S(1)} %pad_maximum_fusion.3), channel_id=1, source_target_pairs={{0,16},{4,20},{8,24},{12,28},{16,0},{20,4},{24,8},{28,12},{1,17},{... | collective-permute-start | bytes 18440 | tf_op jit(solution)/shard_map/ppermute | solution.py:517
  171.7 15.7 %collective-permute-start.24 = (bf16[1,384,640]{2,1,0:T(8,128)(2,1)}, bf16[1,384,640]{2,1,0:T(8,128)(2,1)}, u32[]{:S(2)}, u32[]{:S(2)}) collective-permute-start(bf16[1,384,640]{2,1,0:T(8,128)(2,1)} %get-tuple-element.126.refs_4_.refs_12_), channel_id=1, source_target_pairs={{0,8},{4,12},{8,0},{12,4},{16,24},{20,28},{24,16},{28,20},{1,9},{5... | collective-permute-start | bytes 1474568 | tf_op jit(solution)/shard_map/ppermute | solution.py:517
  173.4 2.8 %collective-permute-start.21 = (f32[2,2,384]{2,0,1:T(2,128)S(1)}, f32[2,2,384]{2,0,1:T(2,128)S(1)}, u32[]{:S(2)}, u32[]{:S(2)}) collective-permute-start(f32[2,2,384]{2,0,1:T(2,128)S(1)} %fusion.14), channel_id=1, source_target_pairs={{0,1},{1,0},{2,3},{3,2},{4,5},{5,4},{6,7},{7,6},{8,9},{9,8},{10,11... | collective-permute-start | bytes 18440 | tf_op jit(solution)/shard_map/ppermute | solution.py:520
  176.2 4.2 %collective-permute-start.22 = (f32[2,2,384]{2,0,1:T(2,128)S(1)}, f32[2,2,384]{2,0,1:T(2,128)S(1)}, u32[]{:S(2)}, u32[]{:S(2)}) collective-permute-start(f32[2,2,384]{2,0,1:T(2,128)S(1)} %fusion.24), channel_id=1, source_target_pairs={{0,2},{1,3},{2,0},{3,1},{4,6},{5,7},{6,4},{7,5},{8,10},{9,11},{10,... | collective-permute-start | bytes 18440 | tf_op jit(solution)/shard_map/ppermute | solution.py:520
  177.8 15.0 %collective-permute-start.25 = (bf16[2,384,640]{2,1,0:T(8,128)(2,1)S(1)}, bf16[2,384,640]{2,1,0:T(8,128)(2,1)S(1)}, u32[]{:S(2)}, u32[]{:S(2)}) collective-permute-start(bf16[2,384,640]{2,1,0:T(8,128)(2,1)S(1)} %copy-done), channel_id=1, source_target_pairs={{0,4},{4,0},{8,12},{12,8},{16,20},{20,16},{24,28},{28,24},{1,5},{5... | collective-permute-start | bytes 2949128 | tf_op jit(solution)/shard_map/ppermute | solution.py:517
  187.4 5.8 %copy-start.1 = (bf16[2,384,640]{2,1,0:T(8,128)(2,1)}, bf16[2,384,640]{2,1,0:T(8,128)(2,1)S(1)}, u32[]{:S(2)}) copy-start(bf16[2,384,640]{2,1,0:T(8,128)(2,1)S(1)} %collective-permute-done.23.refs_2_.refs_10_) | copy-start | bytes 2949124
  187.4 5.8 %collective-permute-start.26 = (bf16[2,384,640]{2,1,0:T(8,128)(2,1)S(1)}, bf16[2,384,640]{2,1,0:T(8,128)(2,1)}, u32[]{:S(2)}, u32[]{:S(2)}) collective-permute-start(bf16[2,384,640]{2,1,0:T(8,128)(2,1)S(1)} %collective-permute-done.23.refs_2_.refs_10_), channel_id=1, source_target_pairs={{0,4},{4,0},{8,12},{12,8},{16,20},{20,16},{24,28},{28,24},{1,5},{5... | collective-permute-start | bytes 2949128 | tf_op jit(solution)/shard_map/ppermute | solution.py:517
  188.5 4.2 %collective-permute-start.29 = (bf16[1,384,640]{2,1,0:T(8,128)(2,1)S(1)}, bf16[1,384,640]{2,1,0:T(8,128)(2,1)}, u32[]{:S(2)}, u32[]{:S(2)}) collective-permute-start(bf16[1,384,640]{2,1,0:T(8,128)(2,1)S(1)} %copy-done.7), channel_id=1, source_target_pairs={{0,4},{4,0},{8,12},{12,8},{16,20},{20,16},{24,28},{28,24},{1,5},{5... | collective-permute-start | bytes 1474568 | tf_op jit(solution)/shard_map/ppermute | solution.py:517
  188.6 4.6 %collective-permute-start.30 = (bf16[1,384,640]{2,1,0:T(8,128)(2,1)}, bf16[1,384,640]{2,1,0:T(8,128)(2,1)}, u32[]{:S(2)}, u32[]{:S(2)}) collective-permute-start(bf16[1,384,640]{2,1,0:T(8,128)(2,1)} %collective-permute-done.24.refs_6_.refs_14_), channel_id=1, source_target_pairs={{0,4},{4,0},{8,12},{12,8},{16,20},{20,16},{24,28},{28,24},{1,5},{5... | collective-permute-start | bytes 1474568 | tf_op jit(solution)/shard_map/ppermute | solution.py:517
  189.0 2.5 collective-permute-start.34
  191.5 6.5 %collective-permute-start.35 = (f32[2,384]{1,0:T(2,128)S(1)}, f32[2,384]{1,0:T(2,128)S(1)}, u32[]{:S(2)}, u32[]{:S(2)}) collective-permute-start(f32[2,384]{1,0:T(2,128)S(1)} %collective-permute-done.34), channel_id=1, source_target_pairs={{0,4},{4,0},{8,12},{12,8},{16,20},{20,16},{24,28},{28,24},{1,5},{5... | collective-permute-start | bytes 9224 | tf_op jit(solution)/shard_map/ppermute | solution.py:517
  192.7 19.2 %collective-permute-start.27 = (bf16[1,384,640]{2,1,0:T(8,128)(2,1)}, bf16[1,384,640]{2,1,0:T(8,128)(2,1)S(1)}, u32[]{:S(2)}, u32[]{:S(2)}) collective-permute-start(bf16[1,384,640]{2,1,0:T(8,128)(2,1)} %get-tuple-element.131.refs_4_), channel_id=1, source_target_pairs={{0,4},{4,0},{8,12},{12,8},{16,20},{20,16},{24,28},{28,24},{1,5},{5... | collective-permute-start | bytes 1474568 | tf_op jit(solution)/shard_map/ppermute | solution.py:517
  192.8 0.9 copy-start.2
  192.8 12.6 %collective-permute-start.28 = (bf16[1,384,640]{2,1,0:T(8,128)(2,1)}, bf16[1,384,640]{2,1,0:T(8,128)(2,1)S(1)}, u32[]{:S(2)}, u32[]{:S(2)}) collective-permute-start(bf16[1,384,640]{2,1,0:T(8,128)(2,1)} %get-tuple-element.131.refs_4_), channel_id=1, source_target_pairs={{0,8},{4,12},{8,0},{12,4},{16,24},{20,28},{24,16},{28,20},{1,9},{5... | collective-permute-start | bytes 1474568 | tf_op jit(solution)/shard_map/ppermute | solution.py:517
  196.7 12.6 %collective-permute-start.31 = (bf16[3,128,640]{2,1,0:T(8,128)(2,1)}, bf16[3,128,640]{2,1,0:T(8,128)(2,1)S(1)}, u32[]{:S(2)}, u32[]{:S(2)}) collective-permute-start(bf16[3,128,640]{2,1,0:T(8,128)(2,1)} %get-tuple-element.133), channel_id=1, source_target_pairs={{0,16},{4,20},{8,24},{12,28},{16,0},{20,4},{24,8},{28,12},{1,17},{... | collective-permute-start | bytes 1474568 | tf_op jit(solution)/shard_map/ppermute | solution.py:517
  198.0 1.5 collective-permute-start.33
  205.4 6.7 %copy-start.9 = (bf16[1,384,640]{2,1,0:T(8,128)(2,1)}, bf16[1,384,640]{2,1,0:T(8,128)(2,1)S(1)}, u32[]{:S(2)}) copy-start(bf16[1,384,640]{2,1,0:T(8,128)(2,1)S(1)} %collective-permute-done.28.refs_6_) | copy-start | bytes 1474564
  209.4 2.8 %collective-permute-start.32 = (bf16[1,384,640]{2,1,0:T(8,128)(2,1)S(1)}, bf16[1,384,640]{2,1,0:T(8,128)(2,1)S(1)}, u32[]{:S(2)}, u32[]{:S(2)}) collective-permute-start(bf16[1,384,640]{2,1,0:T(8,128)(2,1)S(1)} %collective-permute-done.28.refs_6_), channel_id=1, source_target_pairs={{0,4},{4,0},{8,12},{12,8},{16,20},{20,16},{24,28},{28,24},{1,5},{5... | collective-permute-start | bytes 1474568 | tf_op jit(solution)/shard_map/ppermute | solution.py:517
  212.0 6.1 %copy-start.13 = (bf16[3,128,640]{2,1,0:T(8,128)(2,1)S(1)}, bf16[3,128,640]{2,1,0:T(8,128)(2,1)}, u32[]{:S(2)}) copy-start(bf16[3,128,640]{2,1,0:T(8,128)(2,1)} %get-tuple-element.148) | copy-start | bytes 1474564
  212.0 0.8 copy-start.8
  212.8 0.8 copy-start.10
  216.8 21.3 %collective-permute-start.37 = (bf16[3,128,640]{2,1,0:T(8,128)(2,1)}, bf16[3,128,640]{2,1,0:T(8,128)(2,1)S(1)}, u32[]{:S(2)}, u32[]{:S(2)}) collective-permute-start(bf16[3,128,640]{2,1,0:T(8,128)(2,1)} %get-tuple-element.147), channel_id=1, source_target_pairs={{0,16},{4,20},{8,24},{12,28},{16,0},{20,4},{24,8},{28,12},{1,17},{... | collective-permute-start | bytes 1474568 | tf_op jit(solution)/shard_map/ppermute | solution.py:517
  229.1 9.0 %copy-start.14 = (bf16[3,128,640]{2,1,0:T(8,128)(2,1)S(1)}, bf16[3,128,640]{2,1,0:T(8,128)(2,1)}, u32[]{:S(2)}) copy-start(bf16[3,128,640]{2,1,0:T(8,128)(2,1)} %get-tuple-element.146) | copy-start | bytes 1474564
  229.1 12.8 %collective-permute-start.36 = (bf16[384,640]{1,0:T(8,128)(2,1)}, bf16[384,640]{1,0:T(8,128)(2,1)S(1)}, u32[]{:S(2)}, u32[]{:S(2)}) collective-permute-start(bf16[384,640]{1,0:T(8,128)(2,1)} %attend.2), channel_id=1, source_target_pairs={{0,16},{4,20},{8,24},{12,28},{16,0},{20,4},{24,8},{28,12},{1,17},{... | collective-permute-start | bytes 1474568 | tf_op jit(solution)/shard_map/ppermute | solution.py:517
  238.3 3.6 %copy-start.12 = (bf16[384,640]{1,0:T(8,128)(2,1)S(1)}, bf16[384,640]{1,0:T(8,128)(2,1)}, u32[]{:S(2)}) copy-start(bf16[384,640]{1,0:T(8,128)(2,1)} %attend.3) | copy-start | bytes 1474564
Sparse Core Ops, SparseCore 0:
  9.6 75.2 all-gather.2
